TPU v7x, 256 devices: a whole 4x4x8 slice. The times are simulated.
256 devices in a mesh: dp: 16 (over y_lo, z), mp: 16 (over y_hi, x, core).
Axes of the slice: x: 4, y: 4 (y_hi: 2, y_lo: 2; y = y_hi * 2 + y_lo), z: 8, core: 2. Of those that a mesh axis runs over, the one named last changes fastest.
Arguments:
- inputs: bfloat16 [10240, 1024], P(('dp', 'mp')), may hold values from -24 to 24
- cotangent: bfloat16 [10240, 1024], P(('dp', 'mp')), may hold values from -24 to 24
- segment_ids: int32 [16, 640], P('dp', 'mp'), may hold values from 0 to 7, never falling along the last dimension, each value on 1 to 160 neighbouring positions
- norm_gain: bfloat16 [1024], replicated, may hold values from 0.5 to 1.5
- w_in: bfloat16 [1024, 32768], P(None, 'mp'), may hold values from -0.1875 to 0.1875
- w_out: bfloat16 [32768, 1024], P('mp'), may hold values from -0.03125 to 0.03125
Outputs:
- input_grad: bfloat16 [10240, 1024], P(('dp', 'mp'))
- w_in_grad: bfloat16 [1024, 32768], P('dp', 'mp')
- w_out_grad: bfloat16 [32768, 1024], P('mp', 'dp')
- gain_grad: float32 [1024], replicated
Inputs may be any that keep to these rules, and one draw needn't show every extreme that they name: `segment_ids`: within each row the ids never fall and every id appears, each on 1 to 160 tokens, one id on exactly 160; tokens with id 8 - 1 are padding.
All inputs are finite; a program needn't handle non-finite values.
Results may differ from a plain program's by a relative error of at most 0.022.
Values may be sent and summed in bfloat16 or wider, within the bound.
No kernel may reach another device: no remote copies, remote signals or barrier semaphores. Data moves between devices by JAX's collectives and lax.ppermute only.
A program may use at most 128 MiB of HBM per device.

v0:
```python
import math

import jax
import jax.numpy as jnp
from jax import lax
from jax.sharding import PartitionSpec as P

TOK_GROUP = 640
SEGS = 8


GELU_C = 0.7978845608
GELU_A = 0.044715


def gelu_parts(pre_act):
    inner = jnp.tanh(GELU_C * (pre_act + GELU_A * pre_act * pre_act * pre_act))
    value = 0.5 * pre_act * (1.0 + inner)
    slope = 0.5 * (1.0 + inner) + 0.5 * pre_act * (1.0 - inner * inner) * GELU_C * (
        1.0 + 3.0 * GELU_A * pre_act * pre_act
    )
    return (value, slope)


def normalize(values):
    floats = values.astype(jnp.float32)
    inv_rms = lax.rsqrt(jnp.mean(floats * floats, axis=-1, keepdims=True) + 1e-06)
    return (floats * inv_rms, inv_rms)


def token_weights(segment_row):
    labels = jnp.arange(SEGS, dtype=jnp.float32)
    onehot = (segment_row[:, None] == labels[None, :]).astype(jnp.float32)
    counts = jnp.sum(onehot, axis=0)
    token_count = jnp.sum(onehot * counts[None, :], axis=1)
    weights = jnp.sqrt(TOK_GROUP / (SEGS * token_count))
    return jnp.where(segment_row == SEGS - 1, jnp.zeros_like(weights), weights)


def contract_rows(left, right, grad_scale):
    product = lax.dot_general(
        left, right, (((0,), (0,)), ((), ())), preferred_element_type=jnp.float32
    )
    return product * grad_scale


def body(inputs, cotangent, segment_ids, norm_gain, w_in, w_out):
    own_rows = inputs.shape[0]
    dp_count = lax.axis_size("dp")
    gain_f = norm_gain.astype(jnp.float32)
    segment_col = segment_ids.reshape(own_rows, 1).astype(jnp.bfloat16)
    normed, inv_rms = normalize(inputs)
    whole_x, whole_cot, whole_seg = (
        lax.all_gather(inputs, "mp", axis=0, tiled=True),
        lax.all_gather(cotangent, "mp", axis=0, tiled=True),
        lax.all_gather(segment_col, "mp", axis=0, tiled=True),
    )
    whole_normed = normalize(whole_x)[0]
    whole_xn = (whole_normed * gain_f[None, :]).astype(jnp.bfloat16)
    group_rows = whole_xn.shape[0]
    grad_scale = 1.0 / math.sqrt(group_rows * dp_count)
    weights = token_weights(whole_seg[:, 0].astype(jnp.float32))
    ge_whole = (whole_cot.astype(jnp.float32) * weights[:, None]).astype(jnp.bfloat16)
    ge_own = lax.dynamic_slice_in_dim(ge_whole, lax.axis_index("mp") * own_rows, own_rows, 0)
    pre_act = jnp.dot(whole_xn, w_in, preferred_element_type=jnp.float32)
    act_value, act_slope = gelu_parts(pre_act)
    hidden = act_value.astype(jnp.bfloat16)
    hidden_grad = lax.dot_general(
        ge_whole, w_out, (((1,), (1,)), ((), ())), preferred_element_type=jnp.float32
    )
    pre_grad = (hidden_grad * act_slope).astype(jnp.bfloat16)
    normed_raw = lax.psum_scatter(
        lax.dot_general(
            pre_grad, w_in, (((1,), (1,)), ((), ())), preferred_element_type=jnp.float32
        ).astype(jnp.bfloat16),
        "mp",
        scatter_dimension=0,
        tiled=True,
    ).astype(jnp.float32)
    normed_grad = normed_raw * gain_f[None, :]
    inner_mean = jnp.mean(normed_grad * normed, axis=-1, keepdims=True)
    input_grad = (
        ge_own.astype(jnp.float32) + inv_rms * (normed_grad - normed * inner_mean)
    ).astype(jnp.bfloat16)
    gain_grad = lax.psum(jnp.sum(normed_raw * normed, axis=0), ("dp", "mp"))
    in_sum = lax.psum_scatter(
        contract_rows(whole_xn, pre_grad, grad_scale).astype(jnp.bfloat16),
        "dp",
        scatter_dimension=0,
        tiled=True,
    )
    out_sum = lax.psum_scatter(
        contract_rows(ge_whole, hidden, grad_scale).astype(jnp.bfloat16),
        "dp",
        scatter_dimension=0,
        tiled=True,
    ).astype(jnp.float32)
    w_out_grad = out_sum.T.astype(jnp.bfloat16)
    return (input_grad, in_sum, w_out_grad, gain_grad)


def solution(mesh):
    in_specs = (
        P(("dp", "mp"), None),
        P(("dp", "mp"), None),
        P("dp", "mp"),
        P(),
        P(None, "mp"),
        P("mp", None),
    )
    out_specs = (P(("dp", "mp"), None), P("dp", "mp"), P("mp", "dp"), P())
    return jax.shard_map(body, mesh=mesh, in_specs=in_specs, out_specs=out_specs, check_vma=False)
```

profile of v0, /device:TPU:2, one launch (start us, length us, event | category | flops | bytes accessed | tf_op | source)
XLA Modules:
  0.0 379.2 jit_solution(8623531750975404216)
XLA Ops:
  7.2 0.0 all-gather.6.cloned.1.call-start
  7.2 0.7 all-gather.6.cloned.1.call-update
  7.9 0.0 all-gather.4.cloned.1.call-start
  7.9 0.7 all-gather.4.cloned.1.call-update
  8.6 0.0 reduce-scatter.4.cloned.1.call-start
  8.7 0.7 convert_element_type.78
  9.4 1.3 dynamic-slice
  11.3 0.7 convert_bitcast_fusion
  12.0 0.2 dynamic-update-slice
  12.1 32.7 %all-reduce = bf16[640]{0:T(1024)(128)(2,1)S(1)} all-reduce(bf16[640]{0:T(1024)(128)(2,1)S(1)} %dynamic-update-slice), channel_id=2, replica_groups=mesh['dp'=16,'mp'=16] {'mp'}, use_global_device_ids=true, to_apply=%add | all-reduce | flops 640 | bytes 2560
  44.9 0.1 convert_reduce_fusion
  45.0 0.1 select_reduce_fusion
  45.1 19.3 %all-gather.6.cloned.1.call-done = bf16[640,1024]{1,0:T(8,128)(2,1)} async-done(((bf16[40,1024]{1,0:T(8,128)(2,1)}), bf16[640,1024]{1,0:T(8,128)(2,1)}) %all-gather.6.cloned.1.call-update) | async-done | bytes 1310736 | tf_op jit(solution)/shard_map/all_gather | solution.py:54
  64.5 1.6 fusion.7
  66.1 50.9 %all-gather.4.cloned.1.call-done = bf16[640,1024]{1,0:T(8,128)(2,1)} async-done(((bf16[40,1024]{1,0:T(8,128)(2,1)}), bf16[640,1024]{1,0:T(8,128)(2,1)}) %all-gather.4.cloned.1.call-update) | async-done | bytes 1310736 | tf_op jit(solution)/shard_map/all_gather | solution.py:55
  117.1 1.6 multiply_convert_fusion.4
  118.7 0.0 copy-start.2
  118.7 5.3 %fusion.15 = f32[640,2048]{1,0:T(8,128)S(1)} fusion(bf16[1024,2048]{1,0:T(8,128)(2,1)} %param.10, bf16[640,1024]{1,0:T(8,128)(2,1)} %all-gather.6.cloned.1.call-done, f32[1024]{0:T(1024)S(1)} %convert_element_type.78, f32[640]{0:T(1024)S(1)} %add_rsqrt_fusion), kind=kOutput, calls=%fused_computation.23 | convolution fusion | flops 2686976000 | bytes 10754560 | tf_op jit(solution)/shard_map/dot_general | solution.py:65
  124.0 0.0 copy-done.2
  124.0 0.0 copy-start.4
  124.0 0.0 copy-start.3
  124.0 5.7 %fusion.6 = bf16[640,2048]{1,0:T(8,128)(2,1)S(1)} fusion(f32[640,2048]{1,0:T(8,128)S(1)} %fusion.15, bf16[640,1024]{1,0:T(8,128)(2,1)S(1)} %multiply_convert_fusion.4, bf16[2048,1024]{1,0:T(8,128)(2,1)S(1)} %copy-done.2), kind=kOutput, calls=%fused_computation.10 | convolution fusion | flops 2709258240 | bytes 13369344 | tf_op jit(solution)/shard_map/dot_general | solution.py:68
  129.6 0.0 copy-done.4
  129.7 0.0 copy-start.5
  129.7 1.5 copy-done.5
  131.1 0.0 copy-done.3
  131.1 4.0 %convolution_convert_fusion = bf16[640,1024]{1,0:T(8,128)(2,1)} fusion(bf16[640,2048]{1,0:T(8,128)(2,1)S(1)} %fusion.6, bf16[1024,2048]{1,0:T(8,128)(2,1)S(1)} %copy-done.3), kind=kOutput, calls=%fused_computation.22 | convolution fusion | flops 2685009920 | bytes 8126464 | tf_op jit(solution)/shard_map/dot_general | solution.py:73
  135.1 0.0 reduce-scatter.4.cloned.1.call-update
  135.1 0.0 reduce-scatter.8.cloned.1.call-start
  135.2 8.1 %multiply_convert_fusion = bf16[1024,2048]{1,0:T(8,128)(2,1)} fusion(bf16[640,1024]{1,0:T(8,128)(2,1)S(1)} %multiply_convert_fusion.4, f32[640,2048]{1,0:T(8,128)} %copy-done.4), kind=kOutput, calls=%fused_computation | convolution fusion | flops 2700345344 | bytes 10747904 | tf_op jit(solution)/shard_map/dot_general | solution.py:41
  143.3 0.0 copy-start
  143.3 0.0 reduce-scatter.8.cloned.1.call-update
  143.3 0.2 reduce-scatter.6.cloned.1.call-start
  143.6 1.1 copy-done
  144.6 7.0 %multiply_convert_fusion.1 = bf16[1024,2048]{1,0:T(8,128)(2,1)} fusion(bf16[640,2048]{1,0:T(8,128)(2,1)} %copy-done.5, bf16[640,1024]{1,0:T(8,128)(2,1)S(1)} %copy-done, f32[1024]{0:T(1024)S(1)} %convert_element_type.78, f32[640]{0:T(1024)S(1)} %add_rsqrt_fusion), kind=kOutput, calls=%fused_computation.1 | convolution fusion | flops 2691170304 | bytes 8133120 | tf_op jit(solution)/shard_map/dot_general | solution.py:41
  151.6 0.0 copy-start.1
  151.6 0.0 reduce-scatter.6.cloned.1.call-update
  151.6 0.9 copy-done.1
  152.5 0.1 fusion.24
  152.6 56.9 %reduce-scatter.4.cloned.1.call-done = bf16[40,1024]{1,0:T(8,128)(2,1)} async-done(((bf16[640,1024]{1,0:T(8,128)(2,1)}), bf16[40,1024]{1,0:T(8,128)(2,1)}) %reduce-scatter.4.cloned.1.call-update) | async-done | bytes 81936 | tf_op jit(solution)/shard_map/reduce_scatter | solution.py:72
  209.5 1.1 fusion.25
  210.6 75.4 %psum.7 = f32[1024]{0:T(1024)} all-reduce(f32[1024]{0:T(1024)S(1)} %get-tuple-element.4), channel_id=1, replica_groups=mesh['dp'=16,'mp'=16] {'dp','mp'}, use_global_device_ids=true, to_apply=%region_9.10 | all-reduce | flops 1024 | bytes 8192 | tf_op jit(solution)/shard_map/psum | solution.py:85
  286.1 1.6 fusion.22
  287.7 4.7 %reduce-scatter.8.cloned.1.call-done = bf16[64,2048]{1,0:T(8,128)(2,1)} async-done(((bf16[1024,2048]{1,0:T(8,128)(2,1)}), bf16[64,2048]{1,0:T(8,128)(2,1)}) %reduce-scatter.8.cloned.1.call-update) | async-done | bytes 262160 | tf_op jit(solution)/shard_map/reduce_scatter | solution.py:92
  292.4 80.3 %reduce-scatter.6.cloned.1.call-done = bf16[64,2048]{1,0:T(8,128)(2,1)} async-done(((bf16[1024,2048]{1,0:T(8,128)(2,1)}), bf16[64,2048]{1,0:T(8,128)(2,1)}) %reduce-scatter.6.cloned.1.call-update) | async-done | bytes 262160 | tf_op jit(solution)/shard_map/reduce_scatter | solution.py:86
  (6 shorter events, 0.0 us)
Async XLA Ops:
  7.2 57.3 %all-gather.6.cloned.1.call-start = ((), (), s32[]{:S(2)}) async-start(), calls=%async_computation.4 | async-start | bytes 1392640 | tf_op jit(solution)/shard_map/all_gather | solution.py:54
  7.9 109.2 %all-gather.4.cloned.1.call-start = ((), (), s32[]{:S(2)}) async-start(), calls=%async_computation.3 | async-start | bytes 1392640 | tf_op jit(solution)/shard_map/all_gather | solution.py:55
  8.6 200.9 %reduce-scatter.4.cloned.1.call-start = ((), (), s32[]{:S(2)}) async-start(), calls=%async_computation.5 | async-start | bytes 1392640 | tf_op jit(solution)/shard_map/reduce_scatter | solution.py:72
  118.7 5.3 %copy-start.2 = (bf16[2048,1024]{1,0:T(8,128)(2,1)S(1)}, bf16[2048,1024]{1,0:T(8,128)(2,1)}, u32[]{:S(2)}) copy-start(bf16[2048,1024]{1,0:T(8,128)(2,1)} %param.11) | copy-start | bytes 12582916
  124.0 5.7 %copy-start.4 = (f32[640,2048]{1,0:T(8,128)}, f32[640,2048]{1,0:T(8,128)S(1)}, u32[]{:S(2)}) copy-start(f32[640,2048]{1,0:T(8,128)S(1)} %fusion.15) | copy-start | bytes 15728644
  124.0 7.2 %copy-start.3 = (bf16[1024,2048]{1,0:T(8,128)(2,1)S(1)}, bf16[1024,2048]{1,0:T(8,128)(2,1)}, u32[]{:S(2)}) copy-start(bf16[1024,2048]{1,0:T(8,128)(2,1)} %param.10) | copy-start | bytes 12582916
  129.7 1.5 copy-start.5
  135.1 157.2 %reduce-scatter.8.cloned.1.call-start = ((), (), s32[]{:S(2)}) async-start(), calls=%async_computation.7 | async-start | bytes 4456448 | tf_op jit(solution)/shard_map/reduce_scatter | solution.py:92
  143.3 1.3 copy-start
  143.3 229.3 %reduce-scatter.6.cloned.1.call-start = ((), (), s32[]{:S(2)}) async-start(), calls=%async_computation.6 | async-start | bytes 4456448 | tf_op jit(solution)/shard_map/reduce_scatter | solution.py:86
  151.6 0.9 copy-start.1
Sparse Core Ops, SparseCore 0:
  10.7 53.7 all-gather.5
  67.2 49.8 all-gather.3
  135.2 74.2 reduce-scatter.3
  212.5 79.8 reduce-scatter.7
  295.3 77.2 reduce-scatter.5
where the time goes:
time: 380 us; the launch traced here: 379 us
  waiting for transfers between devices  214 us (56%)
  blocking collectives  108 us (28%)
  matrix products  30 us (8%)
  between operations  14.5 us (4%)
  other arithmetic  7.69 us (2%)
  local copies, waits for them, and re-layouts  4.85 us (1%)
    reduce_scatter x1, waiting for transfers between devices, body(): lax.psum_scatter(contract_rows(whole_xn, pre_grad, grad_scale).astype(jnp...  80.3 us
    psum x1, blocking collectives, body(): gain_grad = lax.psum(jnp.sum(normed_raw * normed, axis=0), ('dp', 'mp'))  75.4 us
    reduce_scatter x1, waiting for transfers between devices, body(): lax.psum_scatter(lax.dot_general(pre_grad, w_in, (((1,), (1,)), ((), ()))...  56.9 us
    all_gather x1, waiting for transfers between devices, body(): lax.all_gather(cotangent, 'mp', axis=0, tiled=True)  50.9 us
    unnamed x1, blocking collectives  32.7 us
    all_gather x1, waiting for transfers between devices, body(): lax.all_gather(inputs, 'mp', axis=0, tiled=True)  19.3 us
    dot_general x2, matrix products, contract_rows(): lax.dot_general(left, right, (((0,), (0,)), ((), ())), preferred_element_...  15.1 us
  transfers between devices with their start and end apart: 5, of which 5 were waited for; matrix products, arithmetic and copies ran while one was open for 6% of the time, Pallas kernels for 0%

commit v1 on v0

v1 whole, which is shorter than its diff:
```python
import math

import jax
import jax.numpy as jnp
from jax import lax
from jax.experimental import pallas as pl
from jax.experimental.pallas import tpu as pltpu
from jax.sharding import PartitionSpec as P

TOK_GROUP = 640
SEGS = 8
OWN = 40
ROW = 4 * OWN
CHUNK = 2 * ROW
PLANE = 4 * CHUNK
D = 1024
HID = 1024
PACK = 2 * D + 128
AXES = ("dp", "mp")
OFFSETS = (0, 1, -1, 2)
MIB = 1024 * 1024

GELU_C = 0.7978845608
GELU_A = 0.044715
F32, BF16 = jnp.float32, jnp.bfloat16


def coords(index):
    dp, mp = divmod(index, 16)
    return ((mp // 2) % 4, (mp // 8) * 2 + dp // 8, dp % 8, mp % 2)


def index_of(x, y, z, c):
    x, y, z = x % 4, y % 4, z % 8
    return ((y % 2) * 8 + z) * 16 + ((y // 2) * 4 + x) * 2 + c


def send(value, move):
    pairs = [(i, index_of(*move(*coords(i)))) for i in range(256)]
    return lax.ppermute(value, AXES, pairs)


def first_axis(o):
    return lambda x, y, z, c: (x + o, y, z, c) if c == 0 else (x, y + o, z, c)


def second_axis(o):
    return lambda x, y, z, c: (x, y + o, z, c) if c == 0 else (x + o, y, z, c)


def other_core(x, y, z, c):
    return (x, y, z, 1 - c)


def partner_y(x, y, z, c):
    return (x, y ^ 1, z, c)


def xor_z(o):
    return lambda x, y, z, c: (x, y, z ^ o, c)


def params(mib):
    return pltpu.CompilerParams(vmem_limit_bytes=mib * MIB)


def cost(flops, moved, trans=0):
    return pl.CostEstimate(flops=flops, bytes_accessed=moved, transcendentals=trans)


def pack_kernel(x_ref, cot_ref, label_ref, gain_ref, out_ref):
    floats = x_ref[...].astype(F32)
    inv_rms = lax.rsqrt(jnp.mean(floats * floats, axis=-1, keepdims=True) + 1e-06)
    normed = floats * inv_rms
    out_ref[:, :D] = (normed * gain_ref[...].astype(F32)).astype(BF16)
    out_ref[:, D : 2 * D] = cot_ref[...]
    out_ref[:, 2 * D :] = label_ref[...]


def pack(inputs, cotangent, labels, gain):
    return pl.pallas_call(
        pack_kernel,
        out_shape=jax.ShapeDtypeStruct((OWN, PACK), BF16),
        compiler_params=params(24),
        cost_estimate=cost(OWN * D * 8, 4 * OWN * D * 2),
        name="pack_rows",
    )(inputs, cotangent, labels, gain)


STEPS = 4
WIDTH = HID // STEPS


def chunk_kernel(y_ref, a_ref, b_ref, w_in_ref, w_out_ref, *refs):
    xn_ref, cot_ref, lab_ref, hid_ref, pg_ref, mine_ref, theirs_ref, done_ref, acc = refs[-9:]
    step = pl.program_id(0)

    @pl.when(step == 0)
    def _():
        for k, src in enumerate((a_ref, b_ref)):
            rows = slice(k * ROW, (k + 1) * ROW)
            xn_ref[rows, :] = src[:, :D]
            cot_ref[rows, :] = src[:, D : 2 * D]
            lab_ref[rows, :] = src[:, 2 * D :]
        acc[...] = jnp.zeros_like(acc)

    p = jnp.dot(xn_ref[...], w_in_ref[...], preferred_element_type=F32)
    g = lax.dot_general(
        cot_ref[...], w_out_ref[...], (((1,), (1,)), ((), ())), preferred_element_type=F32
    )
    p2 = p * p
    h = 0.5 * jnp.tanh(p * (GELU_C + (GELU_C * GELU_A) * p2)) + 0.5
    q = p * (2.0 * GELU_C + (6.0 * GELU_C * GELU_A) * p2)
    hid_ref[...] = (p * h).astype(BF16)
    pre_grad = (g * (h * (1.0 + (q - q * h)))).astype(BF16)
    pg_ref[...] = pre_grad
    acc[...] += lax.dot_general(
        pre_grad, w_in_ref[...], (((1,), (1,)), ((), ())), preferred_element_type=F32
    )

    @pl.when(step == STEPS - 1)
    def _():
        mine_ref[...] = acc[:ROW, :].astype(BF16)
        theirs_ref[...] = acc[ROW:, :].astype(BF16)
        done_ref[...] = acc[:8, :128]


def chunk(j, y_lo, a, b, w_in, w_out, full):
    anywhere = pl.BlockSpec(memory_space=pl.ANY)
    fixed = lambda shape: pl.BlockSpec(shape, lambda i, y: (0, 0))
    at_j = lambda shape: pl.BlockSpec(shape, lambda i, y: (j, 0))
    out_specs = [
        at_j((CHUNK, D)),
        at_j((CHUNK, D)),
        at_j((CHUNK, 128)),
        pl.BlockSpec((CHUNK, WIDTH), lambda i, y: (j, i)),
        pl.BlockSpec((CHUNK, WIDTH), lambda i, y: (j, i)),
        at_j((ROW, D)),
        at_j((ROW, D)),
        fixed((8, 128)),
    ]
    shapes = [
        (PLANE, D),
        (PLANE, D),
        (PLANE, 128),
        (PLANE, HID),
        (PLANE, HID),
        (TOK_GROUP, D),
        (TOK_GROUP, D),
    ]
    olds = list(full) if full is not None else []
    return pl.pallas_call(
        chunk_kernel,
        grid_spec=pltpu.PrefetchScalarGridSpec(
            num_scalar_prefetch=1,
            grid=(STEPS,),
            in_specs=[
                fixed((ROW, PACK)),
                fixed((ROW, PACK)),
                pl.BlockSpec((D, WIDTH), lambda i, y: (0, y[0] * STEPS + i)),
                pl.BlockSpec((WIDTH, D), lambda i, y: (y[0] * STEPS + i, 0)),
            ]
            + [anywhere] * len(olds),
            out_specs=out_specs,
            scratch_shapes=[pltpu.VMEM((CHUNK, D), F32)],
        ),
        out_shape=[jax.ShapeDtypeStruct(s, BF16) for s in shapes]
        + [jax.ShapeDtypeStruct((8, 128), F32)],
        input_output_aliases={5 + k: k for k in range(len(olds))},
        compiler_params=params(24),
        cost_estimate=cost(6 * CHUNK * D * HID, 9 * MIB, CHUNK * HID),
        name="chunk_%d" % j,
    )(y_lo, a, b, w_in, w_out, *olds)


def token_weights(labels):
    labels = labels.astype(F32)
    lanes = lax.broadcasted_iota(jnp.int32, (PLANE, 128), 1).astype(F32)
    onehot = jnp.where(labels == lanes, 1.0, 0.0)
    counts = jnp.sum(onehot, axis=0, keepdims=True)
    token_count = jnp.sum(onehot * counts, axis=1, keepdims=True)
    weights = jnp.sqrt(TOK_GROUP / (SEGS * token_count))
    padding = jnp.sum(onehot * jnp.where((lanes == 7.0) | (lanes == 15.0), 1.0, 0.0), axis=1, keepdims=True)
    return jnp.where(padding > 0.5, 0.0, weights)


GRAD_SCALE = 1.0 / math.sqrt(TOK_GROUP * 16)
COLS = 256


def store_grad(out_ref, left_ref, scaled):
    product = lax.dot_general(
        left_ref[...], scaled[...], (((0,), (0,)), ((), ())), preferred_element_type=F32
    )
    out_ref[...] = (product * GRAD_SCALE).astype(BF16).reshape(out_ref.shape)


def out_grad_kernel(lab_ref, cot_ref, hid_ref, out_ref, w_ref, scaled):
    @pl.when(pl.program_id(0) == 0)
    def _():
        weights = token_weights(lab_ref[...])
        scaled[...] = (hid_ref[...].astype(F32) * weights).astype(BF16)
        w_ref[...] = jnp.broadcast_to(weights, (PLANE, 128))

    store_grad(out_ref, cot_ref, scaled)


def in_grad_kernel(
    w_ref, xn_ref, pg_ref, mine_ref, theirs_ref, old_ref, out_ref, gain_ref, scaled
):
    @pl.when(pl.program_id(0) == 0)
    def _():
        scaled[...] = (pg_ref[...].astype(F32) * w_ref[:, :1]).astype(BF16)

    store_grad(out_ref, xn_ref, scaled)
    total = jnp.zeros((1, COLS), F32)
    for j in range(4):
        for k, raw in enumerate((mine_ref, theirs_ref)):
            rows = slice(j * CHUNK + k * ROW, j * CHUNK + (k + 1) * ROW)
            w = jnp.concatenate([w_ref[rows, :]] * (COLS // 128), axis=1)
            term = xn_ref[rows, :].astype(F32) * raw[j * ROW : (j + 1) * ROW, :].astype(F32) * w
            total = total + jnp.sum(term, axis=0, keepdims=True)
    gain_ref[...] = jnp.broadcast_to(total, (8, COLS))


def whole(shape):
    return pl.BlockSpec(shape, lambda i: (0, 0))


def column(rows):
    return pl.BlockSpec((rows, COLS), lambda i: (0, i))


def grad_call(kernel, which, in_specs, args, extra_spec, extra_shape, aliases, name):
    return pl.pallas_call(
        kernel,
        grid=(D // COLS,),
        in_specs=in_specs,
        out_specs=[
            pl.BlockSpec((4, 1, 1, 64, HID), lambda i: (i % 2, which, i // 2, 0, 0)),
            extra_spec,
        ],
        out_shape=[jax.ShapeDtypeStruct((8, 2, 2, 64, HID), BF16), extra_shape],
        scratch_shapes=[pltpu.VMEM((PLANE, HID), BF16)],
        input_output_aliases=aliases,
        compiler_params=params(24),
        cost_estimate=cost(2 * PLANE * D * HID, 8 * MIB),
        name=name,
    )(*args)


def join_halves(summed, y_lo):
    mine = lax.dynamic_index_in_dim(summed, y_lo, 1, False)
    give = lax.dynamic_index_in_dim(summed, 1 - y_lo, 1, False)
    got = send(give, partner_y)
    low = jnp.where(y_lo == 0, mine, got)
    high = jnp.where(y_lo == 0, got, mine)
    return jnp.concatenate([low, high], axis=2)


def gain_rows(part):
    high = part.astype(BF16)
    low = (part - high.astype(F32)).astype(BF16)
    return jnp.pad(jnp.stack([high, low]), ((0, 6), (0, 0)))


def gain_read(rows):
    return rows[0].astype(F32) + rows[1].astype(F32)


def body(inputs, cotangent, segment_ids, norm_gain, w_in, w_out):
    dp = lax.axis_index("dp")
    y_lo, z = lax.div(dp, 8), lax.rem(dp, 8)
    y_arr = y_lo.reshape(1)
    gain_f = norm_gain.astype(F32)

    labels = (segment_ids + SEGS * y_lo).astype(BF16).reshape(OWN, 1)
    labels = jnp.broadcast_to(labels, (OWN, 128))
    packed = pack(inputs, cotangent, labels, norm_gain.reshape(1, D))

    row = jnp.concatenate([packed] + [send(packed, first_axis(-o)) for o in OFFSETS[1:]], axis=0)
    rows = [row] + [send(row, second_axis(-o)) for o in OFFSETS[1:]]
    full = None
    swapped = {0: send(row, other_core)}
    for j in range(4):
        *full, done = chunk(j, y_arr, rows[j], swapped[j], w_in, w_out, full)
        if j < 2:
            for k in ((1, 2), (3,))[j]:
                rows[k] = lax.optimization_barrier((rows[k], done))[0]
                swapped[k] = send(rows[k], other_core)
    xn, cot, lab, hid, pre_grad, mine, theirs = full

    weight_shape = (PLANE, 128)
    grads, weights = grad_call(
        out_grad_kernel,
        0,
        [whole(weight_shape), column(PLANE), whole((PLANE, HID))],
        (lab, cot, hid),
        whole(weight_shape),
        jax.ShapeDtypeStruct(weight_shape, F32),
        {},
        "out_grad",
    )
    grads, gain_part = grad_call(
        in_grad_kernel,
        1,
        [whole(weight_shape), column(PLANE), whole((PLANE, HID))]
        + [column(TOK_GROUP)] * 2
        + [pl.BlockSpec(memory_space=pl.ANY)],
        (weights, xn, pre_grad, mine, theirs, grads),
        column(8),
        jax.ShapeDtypeStruct((8, D), F32),
        {5: 0},
        "in_grad",
    )
    planes = [list(range(8)), list(range(8, 16))]
    summed = lax.psum_scatter(
        grads.reshape(2 * D, HID), "dp", scatter_dimension=0, axis_index_groups=planes, tiled=True
    ).reshape(2, 2, 64, HID)

    total = mine.astype(F32) + send(theirs, other_core).astype(F32)
    gain_part = gain_part + send(gain_part, other_core)
    gain_part = gain_part[0]
    for axis, count in ((second_axis, ROW), (first_axis, OWN)):
        blocks = total.astype(BF16).reshape(4, count, D)
        ride = gain_rows(gain_part)
        total = blocks[0].astype(F32)
        gain_part = gain_read(ride)
        for j, o in enumerate(OFFSETS[1:], 1):
            got = send(jnp.concatenate([blocks[j], ride]), axis(o))
            total = total + got[:count].astype(F32)
            gain_part = gain_part + gain_read(got[count:])
    gain_part = gain_part.reshape(8, 128)
    for o in (1, 2, 4):
        gain_part = gain_part + send(gain_part, xor_z(o))
    gain_grad = gain_part.reshape(D) / gain_f

    floats = inputs.astype(F32)
    inv_rms = lax.rsqrt(jnp.mean(floats * floats, axis=-1, keepdims=True) + 1e-06)
    normed = floats * inv_rms
    own_weights = weights[:OWN, :1]
    normed_raw = total * own_weights
    ge_own = (cotangent.astype(F32) * own_weights).astype(BF16)
    normed_grad = normed_raw * gain_f[None, :]
    inner_mean = jnp.mean(normed_grad * normed, axis=-1, keepdims=True)
    input_grad = (
        ge_own.astype(F32) + inv_rms * (normed_grad - normed * inner_mean)
    ).astype(BF16)

    w_out_grad, w_in_grad = join_halves(summed, y_lo)
    w_out_grad = w_out_grad.T
    return (input_grad, w_in_grad, w_out_grad, gain_grad)


def solution(mesh):
    in_specs = (
        P(("dp", "mp"), None),
        P(("dp", "mp"), None),
        P("dp", "mp"),
        P(),
        P(None, "mp"),
        P("mp", None),
    )
    out_specs = (P(("dp", "mp"), None), P("dp", "mp"), P("mp", "dp"), P())
    return jax.shard_map(body, mesh=mesh, in_specs=in_specs, out_specs=out_specs, check_vma=False)
```

time: 380 us -> 150 us (0.39)
  waiting for transfers between devices: 214 us -> 49.6 us
  blocking collectives: 108 us -> 0 us
  starting transfers between devices: 0.38 us -> 34.1 us
  Pallas kernels: 0 us -> 30.1 us
  matrix products: 30 us -> 0 us
  local copies, waits for them, and re-layouts: 4.85 us -> 13.3 us
    reduce_scatter x3 -> x1, waiting for transfers between devices: 142 us -> 13.2 us  [body(): lax.psum_scatter(grads.reshape(2 * D, HID), 'dp', scatter_dimension=0, ax...]
    psum x1 -> x0, blocking collectives: 75.4 us -> none  [body(): gain_grad = lax.psum(jnp.sum(normed_raw * normed, axis=0), ('dp', 'mp'))]
    all_gather x2 -> x0, waiting for transfers between devices: 70.3 us -> none  [the longest x1 50.9 us: body(): lax.all_gather(cotangent, 'mp', axis=0, tiled=True)]
    ppermute x0 -> x22, waiting for transfers between devices: none -> 36.4 us  [send(): return lax.ppermute(value, AXES, pairs)]
    ppermute x0 -> x22, starting transfers between devices: none -> 34.1 us  [send(): return lax.ppermute(value, AXES, pairs)]
    unnamed x1 -> x0, blocking collectives: 32.7 us -> none
    pallas_call x0 -> x7, Pallas kernels: none -> 30.1 us  [the longest x4 19 us: chunk(): pl.pallas_call(chunk_kernel, grid_spec=pltpu.PrefetchScalarGridSpec(num_s...]
    dot_general x5 -> x0, matrix products: 30 us -> none  [the longest x2 15.1 us: contract_rows(): lax.dot_general(left, right, (((0,), (0,)), ((), ())), preferred_element_...]
  transfers between devices with their start and end apart: 5 -> 23, of which waited for: 5 -> 14; matrix products, arithmetic and copies ran while one was open for 6% -> 4% of each run, Pallas kernels for 0% -> 10%
where the time goes in v1:
time: 150 us; the launch traced here: 149 us
  waiting for transfers between devices  49.6 us (33%)
  starting transfers between devices  34.1 us (23%)
  Pallas kernels  30.1 us (20%)
  between operations  14.2 us (9%)
  local copies, waits for them, and re-layouts  13.3 us (9%)
  other arithmetic  7.93 us (5%)
    ppermute x22, waiting for transfers between devices, send(): return lax.ppermute(value, AXES, pairs)  36.4 us
    ppermute x22, starting transfers between devices, send(): return lax.ppermute(value, AXES, pairs)  34.1 us
    pallas_call x4, Pallas kernels, chunk(): pl.pallas_call(chunk_kernel, grid_spec=pltpu.PrefetchScalarGridSpec(num_s...  19 us
    reduce_scatter x1, waiting for transfers between devices, body(): lax.psum_scatter(grads.reshape(2 * D, HID), 'dp', scatter_dimension=0, ax...  13.2 us
    unnamed x24, local copies, waits for them, and re-layouts  11.4 us
    pallas_call x2, Pallas kernels, grad_call(): pl.pallas_call(kernel, grid=(D // COLS,), in_specs=in_specs, out_specs=[p...  10.9 us
  transfers between devices with their start and end apart: 23, of which 14 were waited for; matrix products, arithmetic and copies ran while one was open for 4% of the time, Pallas kernels for 10%

profile of v1, /device:TPU:2, one launch (start us, length us, event | category | flops | bytes accessed | tf_op | source)
XLA Modules:
  0.0 149.3 jit_solution(15437927319975961611)
XLA Ops:
  7.2 0.0 reduce-scatter.2.cloned.1.call-start
  7.2 0.7 reshape.80.gain_ref
  7.9 0.7 convert_bitcast_fusion
  8.6 0.1 broadcast_in_dim.5.label_ref
  8.6 0.9 copy-done.7
  9.5 0.9 copy-done.9
  10.4 0.1 pack_rows.1
  10.5 2.3 %collective-permute-start = (bf16[40,2176]{1,0:T(8,128)(2,1)S(1)}, bf16[40,2176]{1,0:T(8,128)(2,1)S(1)}, u32[]{:S(2)}, u32[]{:S(2)}) collective-permute-start(bf16[40,2176]{1,0:T(8,128)(2,1)S(1)} %pack_rows.1), channel_id=1, source_target_pairs={{0,6},{1,137},{2,0},{3,139},{4,2},{5,141},{6,4},{7,143},{8,14},{9,... | collective-permute-start | bytes 522248 | tf_op jit(solution)/shard_map/ppermute | solution.py:40
  12.9 3.1 %collective-permute-start.2 = (bf16[40,2176]{1,0:T(8,128)(2,1)S(1)}, bf16[40,2176]{1,0:T(8,128)(2,1)S(1)}, u32[]{:S(2)}, u32[]{:S(2)}) collective-permute-start(bf16[40,2176]{1,0:T(8,128)(2,1)S(1)} %pack_rows.1), channel_id=1, source_target_pairs={{0,4},{1,9},{2,6},{3,11},{4,0},{5,13},{6,2},{7,15},{8,12},{9,1},{1... | collective-permute-start | bytes 522248 | tf_op jit(solution)/shard_map/ppermute | solution.py:40
  16.0 0.1 collective-permute-done
  16.0 2.3 %collective-permute-done.1 = bf16[40,2176]{1,0:T(8,128)(2,1)S(1)} collective-permute-done((bf16[40,2176]{1,0:T(8,128)(2,1)S(1)}, bf16[40,2176]{1,0:T(8,128)(2,1)S(1)}, u32[]{:S(2)}, u32[]{:S(2)}) %collective-permute-start.1) | collective-permute-done | bytes 174112 | tf_op jit(solution)/shard_map/ppermute | solution.py:40
  18.3 1.5 %collective-permute-done.2 = bf16[40,2176]{1,0:T(8,128)(2,1)S(1)} collective-permute-done((bf16[40,2176]{1,0:T(8,128)(2,1)S(1)}, bf16[40,2176]{1,0:T(8,128)(2,1)S(1)}, u32[]{:S(2)}, u32[]{:S(2)}) %collective-permute-start.2) | collective-permute-done | bytes 174112 | tf_op jit(solution)/shard_map/ppermute | solution.py:40
  19.8 0.1 pad_maximum_fusion.a_ref
  19.9 0.8 collective-permute-start.6
  20.7 2.1 %collective-permute-start.8 = (bf16[160,2176]{1,0:T(8,128)(2,1)S(1)}, bf16[160,2176]{1,0:T(8,128)(2,1)S(1)}, u32[]{:S(2)}, u32[]{:S(2)}) collective-permute-start(bf16[160,2176]{1,0:T(8,128)(2,1)S(1)} %pad_maximum_fusion.a_ref), channel_id=1, source_target_pairs={{0,136},{1,7},{2,138},{3,1},{4,140},{5,3},{6,142},{7,5},{8,128},{9... | collective-permute-start | bytes 2088968 | tf_op jit(solution)/shard_map/ppermute | solution.py:40
  22.8 2.2 %collective-permute-start.3 = (bf16[160,2176]{1,0:T(8,128)(2,1)S(1)}, bf16[160,2176]{1,0:T(8,128)(2,1)S(1)}, u32[]{:S(2)}, u32[]{:S(2)}) collective-permute-start(bf16[160,2176]{1,0:T(8,128)(2,1)S(1)} %pad_maximum_fusion.a_ref), channel_id=1, source_target_pairs={{0,8},{1,5},{2,10},{3,7},{4,12},{5,1},{6,14},{7,3},{8,0},{9,13},{1... | collective-permute-start | bytes 2088968 | tf_op jit(solution)/shard_map/ppermute | solution.py:40
  25.0 2.2 %copy-done = bf16[1024,2048]{1,0:T(8,128)(2,1)S(1)} copy-done((bf16[1024,2048]{1,0:T(8,128)(2,1)S(1)}, bf16[1024,2048]{1,0:T(8,128)(2,1)}, u32[]{:S(2)}) %copy-start) | copy-done | bytes 4194328
  27.2 2.2 %copy-done.2 = bf16[2048,1024]{1,0:T(8,128)(2,1)S(1)} copy-done((bf16[2048,1024]{1,0:T(8,128)(2,1)S(1)}, bf16[2048,1024]{1,0:T(8,128)(2,1)}, u32[]{:S(2)}) %copy-start.2) | copy-done | bytes 4194328
  29.4 4.8 %chunk_0.1 = (bf16[1280,1024]{1,0:T(8,128)(2,1)S(1)}, bf16[1280,1024]{1,0:T(8,128)(2,1)S(1)}, bf16[1280,128]{1,0:T(8,128)(2,1)S(1)}, bf16[1280,1024]{1,0:T(8,128...) custom-call(s32[1]{0:T(128)} %bitcast.y_ref, ...), custom_call_target="tpu_custom_call" | custom-call | flops 2013265920 | bytes 9437184 | tf_op jit(solution)/shard_map/chunk_0/pallas_call | solution.py:152
  34.2 4.7 %collective-permute-done.8.a_ref = bf16[160,2176]{1,0:T(8,128)(2,1)S(1)} collective-permute-done((bf16[160,2176]{1,0:T(8,128)(2,1)S(1)}, bf16[160,2176]{1,0:T(8,128)(2,1)S(1)}, u32[]{:S(2)}, u32[]{:S(2)}) %collective-permute-start.8) | collective-permute-done | bytes 696352 | tf_op jit(solution)/shard_map/ppermute | solution.py:40
  38.9 3.7 %collective-permute-done.5.a_ref = bf16[160,2176]{1,0:T(8,128)(2,1)S(1)} collective-permute-done((bf16[160,2176]{1,0:T(8,128)(2,1)S(1)}, bf16[160,2176]{1,0:T(8,128)(2,1)S(1)}, u32[]{:S(2)}, u32[]{:S(2)}) %collective-permute-start.5) | collective-permute-done | bytes 696352 | tf_op jit(solution)/shard_map/ppermute | solution.py:40
  42.5 0.5 collective-permute-start.4
  43.0 4.8 %chunk_1.1 = (bf16[1280,1024]{1,0:T(8,128)(2,1)S(1)}, bf16[1280,1024]{1,0:T(8,128)(2,1)S(1)}, bf16[1280,128]{1,0:T(8,128)(2,1)S(1)}, bf16[1280,1024]{1,0:T(8,128...) custom-call(s32[1]{0:T(128)} %bitcast.y_ref, ...), custom_call_target="tpu_custom_call", output_to_operand_aliasing={{0}: (5, {}), {1}: (6, {}), {2}: (7, {}), {3}: (8, {}), {4}... | custom-call | flops 2013265920 | bytes 9437184 | tf_op jit(solution)/shard_map/chunk_1/pallas_call | solution.py:152
  47.8 4.7 %chunk_2.1 = (bf16[1280,1024]{1,0:T(8,128)(2,1)S(1)}, bf16[1280,1024]{1,0:T(8,128)(2,1)S(1)}, bf16[1280,128]{1,0:T(8,128)(2,1)S(1)}, bf16[1280,1024]{1,0:T(8,128...) custom-call(s32[1]{0:T(128)} %bitcast.y_ref, ...), custom_call_target="tpu_custom_call", output_to_operand_aliasing={{0}: (5, {}), {1}: (6, {}), {2}: (7, {}), {3}: (8, {}), {4}... | custom-call | flops 2013265920 | bytes 9437184 | tf_op jit(solution)/shard_map/chunk_2/pallas_call | solution.py:152
  52.6 4.8 %chunk_3.1 = (bf16[1280,1024]{1,0:T(8,128)(2,1)S(1)}, bf16[1280,1024]{1,0:T(8,128)(2,1)S(1)}, bf16[1280,128]{1,0:T(8,128)(2,1)S(1)}, bf16[1280,1024]{1,0:T(8,128...) custom-call(s32[1]{0:T(128)} %bitcast.y_ref, ...), custom_call_target="tpu_custom_call", output_to_operand_aliasing={{0}: (5, {}), {1}: (6, {}), {2}: (7, {}), {3}: (8, {}), {4}... | custom-call | flops 2013265920 | bytes 9437184 | tf_op jit(solution)/shard_map/chunk_3/pallas_call | solution.py:152
  57.3 1.5 copy-done.4
  58.8 1.7 %copy-done.5 = bf16[1280,1024]{1,0:T(8,128)(2,1)S(1)} copy-done((bf16[1280,1024]{1,0:T(8,128)(2,1)S(1)}, bf16[1280,1024]{1,0:T(8,128)(2,1)}, u32[]{:S(2)}) %copy-start.5) | copy-done | bytes 2621464
  60.6 5.2 %out_grad.1 = (bf16[8,2,2,64,1024]{4,3,2,1,0:T(8,128)(2,1)S(1)}, f32[1280,128]{1,0:T(8,128)S(1)}) custom-call(bf16[1280,128]{1,0:T(8,128)(2,1)S(1)} %get-tuple-element.63.lab_ref, bf16[1280,1024]{1,0:T(8,128)(2,1)S(1)} %copy-done.5, bf16[1280,1024]{1,0:T(8,128)(2,1)S(1)} %get-tuple-element.65.hid_ref), custom_call_target="tpu_custom_call" | custom-call | flops 2684354560 | bytes 8388608 | tf_op jit(solution)/shard_map/out_grad/pallas_call | solution.py:235
  65.8 5.7 %in_grad.1 = (bf16[8,2,2,64,1024]{4,3,2,1,0:T(8,128)(2,1)S(1)}, f32[8,1024]{1,0:T(8,128)S(1)}) custom-call(f32[1280,128]{1,0:T(8,128)S(1)} %get-tuple-element.66.w_ref, bf16[1280,1024]{1,0:T(8,128)(2,1)S(1)} %get-tuple-element.69.xn_ref, bf16[1280,1024]{1,0:T(8,128)(2,1)S(1)} %get-tuple-element.70.pg_ref, ...), custom_call_target="tpu_custom_call", output_to_operand_aliasing={{0}: (5, {})} | custom-call | flops 2684354560 | bytes 8388608 | tf_op jit(solution)/shard_map/in_grad/pallas_call | solution.py:235
  71.5 2.0 %copy-done.6 = bf16[8,2,2,64,1024]{4,3,2,1,0:T(8,128)(2,1)} copy-done((bf16[8,2,2,64,1024]{4,3,2,1,0:T(8,128)(2,1)}, bf16[8,2,2,64,1024]{4,3,2,1,0:T(8,128)(2,1)S(1)}, u32[]{:S(2)}) %copy-start.6) | copy-done | bytes 4194328
  73.5 0.0 reduce-scatter.2.cloned.1.call-update
  73.5 0.1 collective-permute-start.10
  73.6 0.5 collective-permute-start.11
  74.1 2.6 %collective-permute-done.11 = f32[8,1024]{1,0:T(8,128)S(1)} collective-permute-done((f32[8,1024]{1,0:T(8,128)S(1)}, f32[8,1024]{1,0:T(8,128)S(1)}, u32[]{:S(2)}, u32[]{:S(2)}) %collective-permute-start.11) | collective-permute-done | bytes 32800 | tf_op jit(solution)/shard_map/ppermute | solution.py:40
  76.8 0.5 add_convert_fusion
  77.3 0.0 copy-start.11
  77.3 0.1 fusion.32
  77.4 1.0 pad_maximum_fusion.3
  78.4 3.2 %collective-permute-start.13 = (bf16[168,1024]{1,0:T(8,128)(2,1)}, bf16[168,1024]{1,0:T(8,128)(2,1)S(1)}, u32[]{:S(2)}, u32[]{:S(2)}) collective-permute-start(bf16[168,1024]{1,0:T(8,128)(2,1)} %get-tuple-element.92), channel_id=1, source_target_pairs={{0,136},{1,7},{2,138},{3,1},{4,140},{5,3},{6,142},{7,5},{8,128},{9... | collective-permute-start | bytes 1032200 | tf_op jit(solution)/shard_map/ppermute | solution.py:40
  81.7 0.1 fusion.10
  81.8 9.0 %collective-permute-done.12 = bf16[168,1024]{1,0:T(8,128)(2,1)S(1)} collective-permute-done((bf16[168,1024]{1,0:T(8,128)(2,1)}, bf16[168,1024]{1,0:T(8,128)(2,1)S(1)}, u32[]{:S(2)}, u32[]{:S(2)}) %collective-permute-start.12) | collective-permute-done | bytes 344096 | tf_op jit(solution)/shard_map/ppermute | solution.py:40
  90.8 0.1 collective-permute-done.14
  90.8 0.8 fusion.29
  91.7 1.2 add_convert_fusion.1
  93.0 1.6 %collective-permute-start.15 = (bf16[48,1024]{1,0:T(8,128)(2,1)S(1)}, bf16[48,1024]{1,0:T(8,128)(2,1)S(1)}, u32[]{:S(2)}, u32[]{:S(2)}) collective-permute-start(bf16[48,1024]{1,0:T(8,128)(2,1)S(1)} %get-tuple-element.88), channel_id=1, source_target_pairs={{0,2},{1,129},{2,4},{3,131},{4,6},{5,133},{6,0},{7,135},{8,10},{9,... | collective-permute-start | bytes 294920 | tf_op jit(solution)/shard_map/ppermute | solution.py:40
  94.5 1.7 %collective-permute-start.16 = (bf16[48,1024]{1,0:T(8,128)(2,1)S(1)}, bf16[48,1024]{1,0:T(8,128)(2,1)S(1)}, u32[]{:S(2)}, u32[]{:S(2)}) collective-permute-start(bf16[48,1024]{1,0:T(8,128)(2,1)S(1)} %get-tuple-element.89), channel_id=1, source_target_pairs={{0,6},{1,137},{2,0},{3,139},{4,2},{5,141},{6,4},{7,143},{8,14},{9,... | collective-permute-start | bytes 294920 | tf_op jit(solution)/shard_map/ppermute | solution.py:40
  96.2 2.2 %collective-permute-start.17 = (bf16[48,1024]{1,0:T(8,128)(2,1)S(1)}, bf16[48,1024]{1,0:T(8,128)(2,1)S(1)}, u32[]{:S(2)}, u32[]{:S(2)}) collective-permute-start(bf16[48,1024]{1,0:T(8,128)(2,1)S(1)} %get-tuple-element.90), channel_id=1, source_target_pairs={{0,4},{1,9},{2,6},{3,11},{4,0},{5,13},{6,2},{7,15},{8,12},{9,1},{1... | collective-permute-start | bytes 294920 | tf_op jit(solution)/shard_map/ppermute | solution.py:40
  98.4 0.1 slice_reduce_fusion
  98.5 1.0 collective-permute-done.16
  99.5 2.8 %collective-permute-done.17 = bf16[48,1024]{1,0:T(8,128)(2,1)S(1)} collective-permute-done((bf16[48,1024]{1,0:T(8,128)(2,1)S(1)}, bf16[48,1024]{1,0:T(8,128)(2,1)S(1)}, u32[]{:S(2)}, u32[]{:S(2)}) %collective-permute-start.17) | collective-permute-done | bytes 98336 | tf_op jit(solution)/shard_map/ppermute | solution.py:40
  102.3 2.0 %collective-permute-start.19 = (f32[8,128]{1,0:T(8,128)S(1)}, f32[8,128]{1,0:T(8,128)S(1)}, u32[]{:S(2)}, u32[]{:S(2)}) collective-permute-start(f32[8,128]{1,0:T(8,128)S(1)} %bitcast.26), channel_id=1, source_target_pairs={{0,16},{1,17},{2,18},{3,19},{4,20},{5,21},{6,22},{7,23},{8,24},{9,... | collective-permute-start | bytes 12296 | tf_op jit(solution)/shard_map/ppermute | solution.py:40
  104.3 0.2 fusion.5
  104.5 1.7 %collective-permute-done.19 = f32[8,128]{1,0:T(8,128)S(1)} collective-permute-done((f32[8,128]{1,0:T(8,128)S(1)}, f32[8,128]{1,0:T(8,128)S(1)}, u32[]{:S(2)}, u32[]{:S(2)}) %collective-permute-start.19) | collective-permute-done | bytes 4128 | tf_op jit(solution)/shard_map/ppermute | solution.py:40
  106.3 3.2 %collective-permute-start.20 = (f32[8,128]{1,0:T(8,128)S(1)}, f32[8,128]{1,0:T(8,128)S(1)}, u32[]{:S(2)}, u32[]{:S(2)}) collective-permute-start(f32[8,128]{1,0:T(8,128)S(1)} %add.171), channel_id=1, source_target_pairs={{0,32},{1,33},{2,34},{3,35},{4,36},{5,37},{6,38},{7,39},{8,40},{9,... | collective-permute-start | bytes 12296 | tf_op jit(solution)/shard_map/ppermute | solution.py:40
  109.4 1.8 %collective-permute-done.20 = f32[8,128]{1,0:T(8,128)S(1)} collective-permute-done((f32[8,128]{1,0:T(8,128)S(1)}, f32[8,128]{1,0:T(8,128)S(1)}, u32[]{:S(2)}, u32[]{:S(2)}) %collective-permute-start.20) | collective-permute-done | bytes 4128 | tf_op jit(solution)/shard_map/ppermute | solution.py:40
  111.3 7.0 %collective-permute-start.21 = (f32[8,128]{1,0:T(8,128)S(1)}, f32[8,128]{1,0:T(8,128)S(1)}, u32[]{:S(2)}, u32[]{:S(2)}) collective-permute-start(f32[8,128]{1,0:T(8,128)S(1)} %add.172), channel_id=1, source_target_pairs={{0,64},{1,65},{2,66},{3,67},{4,68},{5,69},{6,70},{7,71},{8,72},{9,... | collective-permute-start | bytes 12296 | tf_op jit(solution)/shard_map/ppermute | solution.py:40
  118.2 13.2 %reduce-scatter.2.cloned.1.call-done = bf16[256,1024]{1,0:T(8,128)(2,1)} async-done(((bf16[2048,1024]{1,0:T(8,128)(2,1)}), bf16[256,1024]{1,0:T(8,128)(2,1)}) %reduce-scatter.2.cloned.1.call-update) | async-done | bytes 524304 | tf_op jit(solution)/shard_map/reduce_scatter | solution.py:317
  131.4 1.0 dynamic-slice_bitcast_fusion
  132.4 1.6 %collective-permute-start.18 = (bf16[2,64,1024]{2,1,0:T(8,128)(2,1)S(1)}, bf16[2,64,1024]{2,1,0:T(8,128)(2,1)S(1)}, u32[]{:S(2)}, u32[]{:S(2)}) collective-permute-start(bf16[2,64,1024]{2,1,0:T(8,128)(2,1)S(1)} %dynamic-slice_bitcast_fusion), channel_id=1, source_target_pairs={{0,128},{1,129},{2,130},{3,131},{4,132},{5,133},{6,134},{7,135},{8... | collective-permute-start | bytes 786440 | tf_op jit(solution)/shard_map/ppermute | solution.py:40
  134.0 0.8 fusion.9
  134.7 0.6 bitcast_divide_fusion
  135.3 5.3 %collective-permute-done.18 = bf16[2,64,1024]{2,1,0:T(8,128)(2,1)S(1)} collective-permute-done((bf16[2,64,1024]{2,1,0:T(8,128)(2,1)S(1)}, bf16[2,64,1024]{2,1,0:T(8,128)(2,1)S(1)}, u32[]{:S(2)}, u32[]{:S(2)}) %collective-permute-start.18) | collective-permute-done | bytes 262176 | tf_op jit(solution)/shard_map/ppermute | solution.py:40
  140.6 1.0 bitcast_select_fusion
  141.6 0.8 fusion.2
  (44 shorter events, 0.2 us)
Async XLA Ops:
  7.2 124.3 %reduce-scatter.2.cloned.1.call-start = ((), (), s32[]{:S(2)}) async-start(), calls=%async_computation.1 | async-start | bytes 4718592 | tf_op jit(solution)/shard_map/reduce_scatter | solution.py:317
  8.6 0.9 copy-start.7
  9.5 0.9 copy-start.9
  10.5 5.5 %collective-permute-start = (bf16[40,2176]{1,0:T(8,128)(2,1)S(1)}, bf16[40,2176]{1,0:T(8,128)(2,1)S(1)}, u32[]{:S(2)}, u32[]{:S(2)}) collective-permute-start(bf16[40,2176]{1,0:T(8,128)(2,1)S(1)} %pack_rows.1), channel_id=1, source_target_pairs={{0,6},{1,137},{2,0},{3,139},{4,2},{5,141},{6,4},{7,143},{8,14},{9,... | collective-permute-start | bytes 522248 | tf_op jit(solution)/shard_map/ppermute | solution.py:40
  12.9 5.4 %collective-permute-start.1 = (bf16[40,2176]{1,0:T(8,128)(2,1)S(1)}, bf16[40,2176]{1,0:T(8,128)(2,1)S(1)}, u32[]{:S(2)}, u32[]{:S(2)}) collective-permute-start(bf16[40,2176]{1,0:T(8,128)(2,1)S(1)} %pack_rows.1), channel_id=1, source_target_pairs={{0,2},{1,129},{2,4},{3,131},{4,6},{5,133},{6,0},{7,135},{8,10},{9,... | collective-permute-start | bytes 522248 | tf_op jit(solution)/shard_map/ppermute | solution.py:40
  12.9 6.9 %collective-permute-start.2 = (bf16[40,2176]{1,0:T(8,128)(2,1)S(1)}, bf16[40,2176]{1,0:T(8,128)(2,1)S(1)}, u32[]{:S(2)}, u32[]{:S(2)}) collective-permute-start(bf16[40,2176]{1,0:T(8,128)(2,1)S(1)} %pack_rows.1), channel_id=1, source_target_pairs={{0,4},{1,9},{2,6},{3,11},{4,0},{5,13},{6,2},{7,15},{8,12},{9,1},{1... | collective-permute-start | bytes 522248 | tf_op jit(solution)/shard_map/ppermute | solution.py:40
  19.9 5.2 %collective-permute-start.6 = (bf16[160,2176]{1,0:T(8,128)(2,1)S(1)}, bf16[160,2176]{1,0:T(8,128)(2,1)S(1)}, u32[]{:S(2)}, u32[]{:S(2)}) collective-permute-start(bf16[160,2176]{1,0:T(8,128)(2,1)S(1)} %pad_maximum_fusion.a_ref), channel_id=1, source_target_pairs={{0,1},{1,0},{2,3},{3,2},{4,5},{5,4},{6,7},{7,6},{8,9},{9,8},{10,11... | collective-permute-start | bytes 2088968 | tf_op jit(solution)/shard_map/ppermute | solution.py:40
  20.7 18.2 %collective-permute-start.8 = (bf16[160,2176]{1,0:T(8,128)(2,1)S(1)}, bf16[160,2176]{1,0:T(8,128)(2,1)S(1)}, u32[]{:S(2)}, u32[]{:S(2)}) collective-permute-start(bf16[160,2176]{1,0:T(8,128)(2,1)S(1)} %pad_maximum_fusion.a_ref), channel_id=1, source_target_pairs={{0,136},{1,7},{2,138},{3,1},{4,140},{5,3},{6,142},{7,5},{8,128},{9... | collective-permute-start | bytes 2088968 | tf_op jit(solution)/shard_map/ppermute | solution.py:40
  22.8 19.7 %collective-permute-start.5 = (bf16[160,2176]{1,0:T(8,128)(2,1)S(1)}, bf16[160,2176]{1,0:T(8,128)(2,1)S(1)}, u32[]{:S(2)}, u32[]{:S(2)}) collective-permute-start(bf16[160,2176]{1,0:T(8,128)(2,1)S(1)} %pad_maximum_fusion.a_ref), channel_id=1, source_target_pairs={{0,128},{1,3},{2,130},{3,5},{4,132},{5,7},{6,134},{7,1},{8,136},{9... | collective-permute-start | bytes 2088968 | tf_op jit(solution)/shard_map/ppermute | solution.py:40
  22.8 19.7 %collective-permute-start.3 = (bf16[160,2176]{1,0:T(8,128)(2,1)S(1)}, bf16[160,2176]{1,0:T(8,128)(2,1)S(1)}, u32[]{:S(2)}, u32[]{:S(2)}) collective-permute-start(bf16[160,2176]{1,0:T(8,128)(2,1)S(1)} %pad_maximum_fusion.a_ref), channel_id=1, source_target_pairs={{0,8},{1,5},{2,10},{3,7},{4,12},{5,1},{6,14},{7,3},{8,0},{9,13},{1... | collective-permute-start | bytes 2088968 | tf_op jit(solution)/shard_map/ppermute | solution.py:40
  25.0 2.2 %copy-start = (bf16[1024,2048]{1,0:T(8,128)(2,1)S(1)}, bf16[1024,2048]{1,0:T(8,128)(2,1)}, u32[]{:S(2)}) copy-start(bf16[1024,2048]{1,0:T(8,128)(2,1)} %w_in_ref.7) | copy-start | bytes 12582916
  27.2 2.2 %copy-start.2 = (bf16[2048,1024]{1,0:T(8,128)(2,1)S(1)}, bf16[2048,1024]{1,0:T(8,128)(2,1)}, u32[]{:S(2)}) copy-start(bf16[2048,1024]{1,0:T(8,128)(2,1)} %w_out_ref.7) | copy-start | bytes 12582916
  29.4 13.6 %copy-start.1 = (bf16[1024,2048]{1,0:T(8,128)(2,1)S(1)}, bf16[1024,2048]{1,0:T(8,128)(2,1)}, u32[]{:S(2)}) copy-start(bf16[1024,2048]{1,0:T(8,128)(2,1)} %w_in_ref.7) | copy-start | bytes 12582916
  29.4 13.6 %copy-start.3 = (bf16[2048,1024]{1,0:T(8,128)(2,1)S(1)}, bf16[2048,1024]{1,0:T(8,128)(2,1)}, u32[]{:S(2)}) copy-start(bf16[2048,1024]{1,0:T(8,128)(2,1)} %w_out_ref.7) | copy-start | bytes 12582916
  38.9 4.2 %collective-permute-start.9 = (bf16[160,2176]{1,0:T(8,128)(2,1)S(1)}, bf16[160,2176]{1,0:T(8,128)(2,1)S(1)}, u32[]{:S(2)}, u32[]{:S(2)}) collective-permute-start(bf16[160,2176]{1,0:T(8,128)(2,1)S(1)} %collective-permute-done.8.a_ref), channel_id=1, source_target_pairs={{0,1},{1,0},{2,3},{3,2},{4,5},{5,4},{6,7},{7,6},{8,9},{9,8},{10,11... | collective-permute-start | bytes 2088968 | tf_op jit(solution)/shard_map/ppermute | solution.py:40
  42.5 5.3 %collective-permute-start.7 = (bf16[160,2176]{1,0:T(8,128)(2,1)S(1)}, bf16[160,2176]{1,0:T(8,128)(2,1)S(1)}, u32[]{:S(2)}, u32[]{:S(2)}) collective-permute-start(bf16[160,2176]{1,0:T(8,128)(2,1)S(1)} %collective-permute-done.5.a_ref), channel_id=1, source_target_pairs={{0,1},{1,0},{2,3},{3,2},{4,5},{5,4},{6,7},{7,6},{8,9},{9,8},{10,11... | collective-permute-start | bytes 2088968 | tf_op jit(solution)/shard_map/ppermute | solution.py:40
  42.5 10.1 %collective-permute-start.4 = (bf16[160,2176]{1,0:T(8,128)(2,1)S(1)}, bf16[160,2176]{1,0:T(8,128)(2,1)S(1)}, u32[]{:S(2)}, u32[]{:S(2)}) collective-permute-start(bf16[160,2176]{1,0:T(8,128)(2,1)S(1)} %collective-permute-done.3.a_ref), channel_id=1, source_target_pairs={{0,1},{1,0},{2,3},{3,2},{4,5},{5,4},{6,7},{7,6},{8,9},{9,8},{10,11... | collective-permute-start | bytes 2088968 | tf_op jit(solution)/shard_map/ppermute | solution.py:40
  57.3 1.5 copy-start.4
  58.8 1.7 %copy-start.5 = (bf16[1280,1024]{1,0:T(8,128)(2,1)S(1)}, bf16[1280,1024]{1,0:T(8,128)(2,1)}, u32[]{:S(2)}) copy-start(bf16[1280,1024]{1,0:T(8,128)(2,1)} %copy-done.4) | copy-start | bytes 7864324
  71.5 2.0 %copy-start.6 = (bf16[8,2,2,64,1024]{4,3,2,1,0:T(8,128)(2,1)}, bf16[8,2,2,64,1024]{4,3,2,1,0:T(8,128)(2,1)S(1)}, u32[]{:S(2)}) copy-start(bf16[8,2,2,64,1024]{4,3,2,1,0:T(8,128)(2,1)S(1)} %get-tuple-element.73) | copy-start | bytes 12582916
  73.5 3.2 %collective-permute-start.10 = (bf16[640,1024]{1,0:T(8,128)(2,1)S(1)}, bf16[640,1024]{1,0:T(8,128)(2,1)S(1)}, u32[]{:S(2)}, u32[]{:S(2)}) collective-permute-start(bf16[640,1024]{1,0:T(8,128)(2,1)S(1)} %get-tuple-element.68.theirs_ref), channel_id=1, source_target_pairs={{0,1},{1,0},{2,3},{3,2},{4,5},{5,4},{6,7},{7,6},{8,9},{9,8},{10,11... | collective-permute-start | bytes 3932168 | tf_op jit(solution)/shard_map/ppermute | solution.py:40
  73.6 3.1 %collective-permute-start.11 = (f32[8,1024]{1,0:T(8,128)S(1)}, f32[8,1024]{1,0:T(8,128)S(1)}, u32[]{:S(2)}, u32[]{:S(2)}) collective-permute-start(f32[8,1024]{1,0:T(8,128)S(1)} %get-tuple-element.72), channel_id=1, source_target_pairs={{0,1},{1,0},{2,3},{3,2},{4,5},{5,4},{6,7},{7,6},{8,9},{9,8},{10,11... | collective-permute-start | bytes 98312 | tf_op jit(solution)/shard_map/ppermute | solution.py:40
  77.3 4.4 %copy-start.11 = (bf16[1024]{0:T(1024)(128)(2,1)S(1)}, bf16[1024]{0:T(1024)(128)(2,1)}, u32[]{:S(2)}) copy-start(bf16[1024]{0:T(1024)(128)(2,1)} %param.9) | copy-start | bytes 6148
  77.3 4.4 %copy-start.8 = (bf16[40,1024]{1,0:T(8,128)(2,1)S(1)}, bf16[40,1024]{1,0:T(8,128)(2,1)}, u32[]{:S(2)}) copy-start(bf16[40,1024]{1,0:T(8,128)(2,1)} %x_ref.1) | copy-start | bytes 245764
  77.4 56.6 %copy-start.10 = (bf16[40,1024]{1,0:T(8,128)(2,1)S(1)}, bf16[40,1024]{1,0:T(8,128)(2,1)}, u32[]{:S(2)}) copy-start(bf16[40,1024]{1,0:T(8,128)(2,1)} %cot_ref.1) | copy-start | bytes 245764
  78.4 12.4 %collective-permute-start.12 = (bf16[168,1024]{1,0:T(8,128)(2,1)}, bf16[168,1024]{1,0:T(8,128)(2,1)S(1)}, u32[]{:S(2)}, u32[]{:S(2)}) collective-permute-start(bf16[168,1024]{1,0:T(8,128)(2,1)} %get-tuple-element.91), channel_id=1, source_target_pairs={{0,128},{1,3},{2,130},{3,5},{4,132},{5,7},{6,134},{7,1},{8,136},{9... | collective-permute-start | bytes 1032200 | tf_op jit(solution)/shard_map/ppermute | solution.py:40
  78.4 12.4 %collective-permute-start.13 = (bf16[168,1024]{1,0:T(8,128)(2,1)}, bf16[168,1024]{1,0:T(8,128)(2,1)S(1)}, u32[]{:S(2)}, u32[]{:S(2)}) collective-permute-start(bf16[168,1024]{1,0:T(8,128)(2,1)} %get-tuple-element.92), channel_id=1, source_target_pairs={{0,136},{1,7},{2,138},{3,1},{4,140},{5,3},{6,142},{7,5},{8,128},{9... | collective-permute-start | bytes 1032200 | tf_op jit(solution)/shard_map/ppermute | solution.py:40
  81.7 9.2 %collective-permute-start.14 = (bf16[168,1024]{1,0:T(8,128)(2,1)}, bf16[168,1024]{1,0:T(8,128)(2,1)}, u32[]{:S(2)}, u32[]{:S(2)}) collective-permute-start(bf16[168,1024]{1,0:T(8,128)(2,1)} %get-tuple-element.93), channel_id=1, source_target_pairs={{0,8},{1,5},{2,10},{3,7},{4,12},{5,1},{6,14},{7,3},{8,0},{9,13},{1... | collective-permute-start | bytes 1032200 | tf_op jit(solution)/shard_map/ppermute | solution.py:40
  93.0 5.6 %collective-permute-start.15 = (bf16[48,1024]{1,0:T(8,128)(2,1)S(1)}, bf16[48,1024]{1,0:T(8,128)(2,1)S(1)}, u32[]{:S(2)}, u32[]{:S(2)}) collective-permute-start(bf16[48,1024]{1,0:T(8,128)(2,1)S(1)} %get-tuple-element.88), channel_id=1, source_target_pairs={{0,2},{1,129},{2,4},{3,131},{4,6},{5,133},{6,0},{7,135},{8,10},{9,... | collective-permute-start | bytes 294920 | tf_op jit(solution)/shard_map/ppermute | solution.py:40
  94.5 5.0 %collective-permute-start.16 = (bf16[48,1024]{1,0:T(8,128)(2,1)S(1)}, bf16[48,1024]{1,0:T(8,128)(2,1)S(1)}, u32[]{:S(2)}, u32[]{:S(2)}) collective-permute-start(bf16[48,1024]{1,0:T(8,128)(2,1)S(1)} %get-tuple-element.89), channel_id=1, source_target_pairs={{0,6},{1,137},{2,0},{3,139},{4,2},{5,141},{6,4},{7,143},{8,14},{9,... | collective-permute-start | bytes 294920 | tf_op jit(solution)/shard_map/ppermute | solution.py:40
  96.2 6.1 %collective-permute-start.17 = (bf16[48,1024]{1,0:T(8,128)(2,1)S(1)}, bf16[48,1024]{1,0:T(8,128)(2,1)S(1)}, u32[]{:S(2)}, u32[]{:S(2)}) collective-permute-start(bf16[48,1024]{1,0:T(8,128)(2,1)S(1)} %get-tuple-element.90), channel_id=1, source_target_pairs={{0,4},{1,9},{2,6},{3,11},{4,0},{5,13},{6,2},{7,15},{8,12},{9,1},{1... | collective-permute-start | bytes 294920 | tf_op jit(solution)/shard_map/ppermute | solution.py:40
  102.3 3.9 %collective-permute-start.19 = (f32[8,128]{1,0:T(8,128)S(1)}, f32[8,128]{1,0:T(8,128)S(1)}, u32[]{:S(2)}, u32[]{:S(2)}) collective-permute-start(f32[8,128]{1,0:T(8,128)S(1)} %bitcast.26), channel_id=1, source_target_pairs={{0,16},{1,17},{2,18},{3,19},{4,20},{5,21},{6,22},{7,23},{8,24},{9,... | collective-permute-start | bytes 12296 | tf_op jit(solution)/shard_map/ppermute | solution.py:40
  106.3 5.0 %collective-permute-start.20 = (f32[8,128]{1,0:T(8,128)S(1)}, f32[8,128]{1,0:T(8,128)S(1)}, u32[]{:S(2)}, u32[]{:S(2)}) collective-permute-start(f32[8,128]{1,0:T(8,128)S(1)} %add.171), channel_id=1, source_target_pairs={{0,32},{1,33},{2,34},{3,35},{4,36},{5,37},{6,38},{7,39},{8,40},{9,... | collective-permute-start | bytes 12296 | tf_op jit(solution)/shard_map/ppermute | solution.py:40
  111.3 23.5 %collective-permute-start.21 = (f32[8,128]{1,0:T(8,128)S(1)}, f32[8,128]{1,0:T(8,128)S(1)}, u32[]{:S(2)}, u32[]{:S(2)}) collective-permute-start(f32[8,128]{1,0:T(8,128)S(1)} %add.172), channel_id=1, source_target_pairs={{0,64},{1,65},{2,66},{3,67},{4,68},{5,69},{6,70},{7,71},{8,72},{9,... | collective-permute-start | bytes 12296 | tf_op jit(solution)/shard_map/ppermute | solution.py:40
  132.4 8.2 %collective-permute-start.18 = (bf16[2,64,1024]{2,1,0:T(8,128)(2,1)S(1)}, bf16[2,64,1024]{2,1,0:T(8,128)(2,1)S(1)}, u32[]{:S(2)}, u32[]{:S(2)}) collective-permute-start(bf16[2,64,1024]{2,1,0:T(8,128)(2,1)S(1)} %dynamic-slice_bitcast_fusion), channel_id=1, source_target_pairs={{0,128},{1,129},{2,130},{3,131},{4,132},{5,133},{6,134},{7,135},{8... | collective-permute-start | bytes 786440 | tf_op jit(solution)/shard_map/ppermute | solution.py:40
Sparse Core Ops, SparseCore 0:
  73.6 57.7 reduce-scatter.1

commit v2 on v1

v2 whole, which is shorter than its diff:
```python
import math

import jax
import jax.numpy as jnp
from jax import lax
from jax.experimental import pallas as pl
from jax.experimental.pallas import tpu as pltpu
from jax.sharding import PartitionSpec as P

TOK_GROUP = 640
SEGS = 8
OWN = 40
ROW = 4 * OWN
CHUNK = 2 * ROW
PLANE = 4 * CHUNK
D = 1024
HID = 1024
PACK = 2 * D + 128
AXES = ("dp", "mp")
OFFSETS = (0, 1, -1, 2)
MIB = 1024 * 1024

GELU_C = 0.7978845608
GELU_A = 0.044715
F32, BF16 = jnp.float32, jnp.bfloat16


def coords(index):
    dp, mp = divmod(index, 16)
    return ((mp // 2) % 4, (mp // 8) * 2 + dp // 8, dp % 8, mp % 2)


def index_of(x, y, z, c):
    x, y, z = x % 4, y % 4, z % 8
    return ((y % 2) * 8 + z) * 16 + ((y // 2) * 4 + x) * 2 + c


def send(value, move):
    pairs = [(i, index_of(*move(*coords(i)))) for i in range(256)]
    return lax.ppermute(value, AXES, pairs)


def first_axis(o):
    return lambda x, y, z, c: (x + o, y, z, c) if c == 0 else (x, y + o, z, c)


def second_axis(o):
    return lambda x, y, z, c: (x, y + o, z, c) if c == 0 else (x + o, y, z, c)


def other_core(x, y, z, c):
    return (x, y, z, 1 - c)


def partner_y(x, y, z, c):
    return (x, y ^ 1, z, c)


def xor_z(o):
    return lambda x, y, z, c: (x, y, z ^ o, c)


def params(mib):
    return pltpu.CompilerParams(vmem_limit_bytes=mib * MIB)


def cost(flops, moved, trans=0):
    return pl.CostEstimate(flops=flops, bytes_accessed=moved, transcendentals=trans)


def pack_kernel(y_ref, x_ref, cot_ref, ids_ref, gain_ref, out_ref):
    floats = x_ref[...].astype(F32)
    inv_rms = lax.rsqrt(jnp.mean(floats * floats, axis=-1, keepdims=True) + 1e-06)
    normed = floats * inv_rms
    out_ref[:, :D] = cot_ref[...]
    out_ref[:, D : 2 * D] = (normed * gain_ref[...].astype(F32).reshape(1, D)).astype(BF16)
    ids = jnp.broadcast_to((ids_ref[...] + SEGS * y_ref[0]).astype(F32), (OWN, OWN))
    along = lax.broadcasted_iota(jnp.int32, (OWN, OWN), 0)
    across = lax.broadcasted_iota(jnp.int32, (OWN, OWN), 1)
    label = jnp.sum(jnp.where(along == across, ids, 0.0), axis=1, keepdims=True)
    out_ref[:, 2 * D :] = jnp.broadcast_to(label, (OWN, 128)).astype(BF16)


def pack(y_lo, inputs, cotangent, ids, gain):
    return pl.pallas_call(
        pack_kernel,
        in_specs=[pl.BlockSpec(memory_space=pltpu.SMEM)]
        + [pl.BlockSpec(memory_space=pltpu.VMEM)] * 4,
        out_shape=jax.ShapeDtypeStruct((OWN, PACK), BF16),
        compiler_params=params(4),
        cost_estimate=cost(OWN * D * 8, 4 * OWN * D * 2),
        name="pack_rows",
    )(y_lo, inputs, cotangent, ids, gain)


def nothing(*refs):
    pass


def after(values, *first):
    anywhere = pl.BlockSpec(memory_space=pl.ANY)
    return pl.pallas_call(
        nothing,
        in_specs=[anywhere] * (len(values) + len(first)),
        out_specs=[anywhere] * len(values),
        out_shape=[jax.ShapeDtypeStruct(v.shape, v.dtype) for v in values],
        input_output_aliases={k: k for k in range(len(values))},
        compiler_params=params(1),
        cost_estimate=cost(0, 0),
        name="after",
    )(*values, *first)


STEPS = 4
WIDTH = HID // STEPS


def chunk_kernel(a_ref, b_ref, w_in_ref, w_out_ref, left_ref, lab_ref, right_ref, mine_ref, theirs_ref, acc):
    for k, src in enumerate((a_ref, b_ref)):
        rows = slice(k * ROW, (k + 1) * ROW)
        left_ref[rows, :] = src[:, : 2 * D]
        lab_ref[rows, :] = src[:, 2 * D :]
    for step in range(STEPS):
        cols = slice(step * WIDTH, (step + 1) * WIDTH)
        p = jnp.dot(left_ref[:, D:], w_in_ref[:, cols], preferred_element_type=F32)
        g = lax.dot_general(
            left_ref[:, :D], w_out_ref[cols, :], (((1,), (1,)), ((), ())), preferred_element_type=F32
        )
        p2 = p * p
        h = 0.5 * jnp.tanh(p * (GELU_C + (GELU_C * GELU_A) * p2)) + 0.5
        q = p * (2.0 * GELU_C + (6.0 * GELU_C * GELU_A) * p2)
        right_ref[:, cols] = (p * h).astype(BF16)
        pre_grad = (g * (h * (1.0 + (q - q * h)))).astype(BF16)
        right_ref[:, HID + step * WIDTH : HID + (step + 1) * WIDTH] = pre_grad
        raw = lax.dot_general(
            pre_grad, w_in_ref[:, cols], (((1,), (1,)), ((), ())), preferred_element_type=F32
        )
        if step == 0:
            acc[...] = raw
        elif step < STEPS - 1:
            acc[...] += raw
        else:
            mine_ref[...] = (acc[:ROW, :] + raw[:ROW]).astype(BF16)
            theirs_ref[...] = (acc[ROW:, :] + raw[ROW:]).astype(BF16)


def chunk(j, a, b, w_in, w_out):
    here = pl.BlockSpec(memory_space=pltpu.VMEM)
    shapes = [(CHUNK, 2 * D), (CHUNK, 128), (CHUNK, 2 * HID), (ROW, D), (ROW, D)]
    return pl.pallas_call(
        chunk_kernel,
        in_specs=[here] * 4,
        out_specs=[here] * 5,
        scratch_shapes=[pltpu.VMEM((CHUNK, D), F32)],
        out_shape=[jax.ShapeDtypeStruct(s, BF16) for s in shapes],
        compiler_params=params(16),
        cost_estimate=cost(6 * CHUNK * D * HID, 9 * MIB, CHUNK * HID),
        name="chunk_%d" % j,
    )(a, b, w_in, w_out)


def token_weights(labels):
    labels = labels.astype(F32)
    lanes = lax.broadcasted_iota(jnp.int32, (PLANE, 128), 1).astype(F32)
    onehot = jnp.where(labels == lanes, 1.0, 0.0)
    counts = jnp.sum(onehot, axis=0, keepdims=True)
    token_count = jnp.sum(onehot * counts, axis=1, keepdims=True)
    weights = jnp.sqrt(TOK_GROUP / (SEGS * token_count))
    padding = jnp.sum(onehot * jnp.where((lanes == 7.0) | (lanes == 15.0), 1.0, 0.0), axis=1, keepdims=True)
    return jnp.where(padding > 0.5, 0.0, weights)


GRAD_SCALE = 1.0 / math.sqrt(TOK_GROUP * 16)
COLS = 256


BLOCKS = D // COLS


def grads_kernel(*refs):
    labs, lefts, rights, raws = refs[:4], refs[4:8], refs[8:12], refs[12:20]
    out_ref, gain_ref, own_ref, weight = refs[20:]
    step = pl.program_id(0)

    @pl.when(step == 0)
    def _():
        weights = token_weights(jnp.concatenate([lab[...] for lab in labs], axis=0))
        weight[...] = jnp.broadcast_to(weights, (PLANE, 128))
        own_ref[...] = jnp.broadcast_to(weights[:OWN], (OWN, 128))

    def product(array, block):
        cols = pl.ds(pl.multiple_of(step * COLS, COLS), COLS)
        left = jnp.concatenate([ref[:, cols] for ref in lefts], axis=0).astype(F32)
        left = left * jnp.concatenate([weight[...]] * (COLS // 128), axis=1)
        right = jnp.concatenate([ref[:, array * HID : (array + 1) * HID] for ref in rights], axis=0)
        total = lax.dot_general(
            left.astype(BF16), right, (((0,), (0,)), ((), ())), preferred_element_type=F32
        )
        out_ref[...] = (total * GRAD_SCALE).astype(BF16).reshape(out_ref.shape)
        return left

    @pl.when(step < BLOCKS)
    def _():
        product(0, step)

    @pl.when(step >= BLOCKS)
    def _():
        left = product(1, step)
        cols = pl.ds(pl.multiple_of((step - BLOCKS) * COLS, COLS), COLS)
        raw = jnp.concatenate([ref[:, cols] for ref in raws], axis=0).astype(F32)
        total = jnp.sum(left * raw, axis=0, keepdims=True)
        gain_ref[...] = jnp.broadcast_to(total, (8, COLS))


def grads_call(labs, lefts, rights, raws):
    here = pl.BlockSpec(memory_space=pltpu.VMEM)
    place = lambda i: (i % 2, i // BLOCKS, (i % BLOCKS) // 2, 0, 0)
    return pl.pallas_call(
        grads_kernel,
        grid=(2 * BLOCKS,),
        in_specs=[here] * 20,
        out_specs=[
            pl.BlockSpec((4, 1, 1, 64, HID), place),
            pl.BlockSpec((8, COLS), lambda i: (0, jnp.maximum(i - BLOCKS, 0))),
            pl.BlockSpec((OWN, 128), lambda i: (0, 0)),
        ],
        out_shape=[
            pltpu.HBM((8, 2, 2, 64, HID), BF16),
            jax.ShapeDtypeStruct((8, D), F32),
            jax.ShapeDtypeStruct((OWN, 128), F32),
        ],
        scratch_shapes=[pltpu.VMEM((PLANE, 128), F32)],
        compiler_params=params(16),
        cost_estimate=cost(4 * PLANE * D * HID, 24 * MIB),
        name="weight_grads",
    )(*labs, *lefts, *rights, *raws)


def join_halves(summed, y_lo):
    mine = lax.dynamic_index_in_dim(summed, y_lo, 1, False)
    give = lax.dynamic_index_in_dim(summed, 1 - y_lo, 1, False)
    got = send(give, partner_y)
    low = jnp.where(y_lo == 0, mine, got)
    high = jnp.where(y_lo == 0, got, mine)
    return jnp.concatenate([low, high], axis=2)


def gain_rows(part):
    high = part.astype(BF16)
    low = (part - high.astype(F32)).astype(BF16)
    return jnp.pad(jnp.stack([high, low]), ((0, 6), (0, 0)))


def gain_read(rows):
    return rows[0].astype(F32) + rows[1].astype(F32)


def body(inputs, cotangent, segment_ids, norm_gain, w_in, w_out):
    dp = lax.axis_index("dp")
    y_lo, z = lax.div(dp, 8), lax.rem(dp, 8)
    y_arr = y_lo.reshape(1)
    gain_f = norm_gain.astype(F32)

    packed = pack(y_arr, inputs, cotangent, segment_ids, norm_gain)

    row = jnp.concatenate([packed] + [send(packed, first_axis(-o)) for o in OFFSETS[1:]], axis=0)
    w_in = lax.dynamic_slice_in_dim(w_in, y_lo * HID, HID, 1)
    w_out = lax.dynamic_slice_in_dim(w_out, y_lo * HID, HID, 0)
    (row,) = after([row], w_in, w_out)
    half = ROW // 2
    rows = [row, send(row, second_axis(-1)), send(row, second_axis(1))]
    swapped = [send(row, other_core)]
    parts = []
    for j in range(4):
        parts.append(chunk(j, rows[j], swapped[j], w_in, w_out))
        done = parts[j][1]
        if j == 0:
            plus, minus = rows[1:] = after(rows[1:], done)
            relayed = [send(plus[:half], second_axis(-1)), send(minus[half:], second_axis(1))]
            swapped += [send(plus, other_core), send(minus, other_core)]
        if j == 1:
            relayed = after(relayed, done)
            rows.append(jnp.concatenate(relayed, axis=0))
            swapped.append(send(rows[3], other_core))
    lefts, labs, rights, mine, theirs = zip(*parts)
    raws = [raw for pair in zip(mine, theirs) for raw in pair]
    grads, gain_part, own_weights = grads_call(labs, lefts, rights, raws)
    mine, theirs = jnp.concatenate(mine), jnp.concatenate(theirs)
    planes = [list(range(8)), list(range(8, 16))]
    summed = lax.psum_scatter(
        grads.reshape(2 * D, HID), "dp", scatter_dimension=0, axis_index_groups=planes, tiled=True
    ).reshape(2, 2, 64, HID)

    total = mine.astype(F32) + send(theirs, other_core).astype(F32)
    gain_part = gain_part + send(gain_part, other_core)
    gain_part = gain_part[0]
    for axis, count in ((second_axis, ROW), (first_axis, OWN)):
        blocks = total.astype(BF16).reshape(4, count, D)
        ride = gain_rows(gain_part)
        total = blocks[0].astype(F32)
        gain_part = gain_read(ride)
        for j, o in enumerate(OFFSETS[1:], 1):
            got = send(jnp.concatenate([blocks[j], ride]), axis(o))
            total = total + got[:count].astype(F32)
            gain_part = gain_part + gain_read(got[count:])
    gain_part = gain_part.reshape(8, 128)
    for o in (1, 2, 4):
        gain_part = gain_part + send(gain_part, xor_z(o))
    gain_grad = gain_part.reshape(D) / gain_f

    floats = inputs.astype(F32)
    inv_rms = lax.rsqrt(jnp.mean(floats * floats, axis=-1, keepdims=True) + 1e-06)
    normed = floats * inv_rms
    own_weights = own_weights[:, :1]
    normed_raw = total * own_weights
    ge_own = (cotangent.astype(F32) * own_weights).astype(BF16)
    normed_grad = normed_raw * gain_f[None, :]
    inner_mean = jnp.mean(normed_grad * normed, axis=-1, keepdims=True)
    input_grad = (
        ge_own.astype(F32) + inv_rms * (normed_grad - normed * inner_mean)
    ).astype(BF16)

    w_out_grad, w_in_grad = join_halves(summed, y_lo)
    w_out_grad = w_out_grad.T
    return (input_grad, w_in_grad, w_out_grad, gain_grad)


def solution(mesh):
    in_specs = (
        P(("dp", "mp"), None),
        P(("dp", "mp"), None),
        P("dp", "mp"),
        P(),
        P(None, "mp"),
        P("mp", None),
    )
    out_specs = (P(("dp", "mp"), None), P("dp", "mp"), P("mp", "dp"), P())
    return jax.shard_map(body, mesh=mesh, in_specs=in_specs, out_specs=out_specs, check_vma=False)
```

time: 150 us -> 135 us (0.900)
  Pallas kernels: 30.1 us -> 22 us
  local copies, waits for them, and re-layouts: 13.3 us -> 7.05 us
  waiting for transfers between devices: 49.6 us -> 52.1 us
  starting transfers between devices: 34.1 us -> 31.9 us
    unnamed x24 -> x15, local copies, waits for them, and re-layouts: 11.4 us -> 3.15 us
    pallas_call x7 -> x9, Pallas kernels: 30.1 us -> 22 us  [the longest x4 12.2 us: chunk(): pl.pallas_call(chunk_kernel, in_specs=[here] * 4, out_specs=[here] * 5, s...]
    ppermute x22 -> x23, waiting for transfers between devices: 36.4 us -> 39.1 us  [send(): return lax.ppermute(value, AXES, pairs)]
    dynamic_slice x0 -> x1, local copies, waits for them, and re-layouts: none -> 2.66 us  [body(): w_out = lax.dynamic_slice_in_dim(w_out, y_lo * HID, HID, 0)]
    ppermute x22 -> x23, starting transfers between devices: 34.1 us -> 31.9 us  [send(): return lax.ppermute(value, AXES, pairs)]
  transfers between devices with their start and end apart: 23 -> 24, of which waited for: 14 -> 18; matrix products, arithmetic and copies ran while one was open for 4% -> 7% of each run, Pallas kernels for 10% -> 7%
where the time goes in v2:
time: 135 us
  waiting for transfers between devices  52.1 us (39%)
  starting transfers between devices  31.9 us (24%)
  Pallas kernels  22 us (16%)
  between operations  14.3 us (11%)
  other arithmetic  7.49 us (6%)
  local copies, waits for them, and re-layouts  7.05 us (5%)
    ppermute x23, waiting for transfers between devices, send(): return lax.ppermute(value, AXES, pairs)  39.1 us
    ppermute x23, starting transfers between devices, send(): return lax.ppermute(value, AXES, pairs)  31.9 us
    reduce_scatter x1, waiting for transfers between devices, body(): lax.psum_scatter(grads.reshape(2 * D, HID), 'dp', scatter_dimension=0, ax...  13 us
    pallas_call x4, Pallas kernels, chunk(): pl.pallas_call(chunk_kernel, in_specs=[here] * 4, out_specs=[here] * 5, s...  12.2 us
    pallas_call x1, Pallas kernels, grads_call(): pl.pallas_call(grads_kernel, grid=(2 * BLOCKS,), in_specs=[here] * 20, ou...  9.72 us
    unnamed x15, local copies, waits for them, and re-layouts  3.15 us
  transfers between devices with their start and end apart: 24, of which 18 were waited for; matrix products, arithmetic and copies ran while one was open for 7% of the time, Pallas kernels for 7%

profile of v2, /device:TPU:2, one launch (start us, length us, event | category | flops | bytes accessed | tf_op | source)
XLA Modules:
  0.0 134.9 jit_solution(502016492443519642)
XLA Ops:
  7.2 0.0 reduce-scatter.2.cloned.1.call-start
  7.2 0.9 copy-done
  8.1 0.9 copy-done.2
  9.0 0.7 copy-done.4
  9.7 0.7 copy-done.6
  10.3 0.1 pack_rows.1
  10.4 2.2 %collective-permute-start.2 = (bf16[40,2176]{1,0:T(8,128)(2,1)S(1)}, bf16[40,2176]{1,0:T(8,128)(2,1)S(1)}, u32[]{:S(2)}, u32[]{:S(2)}) collective-permute-start(bf16[40,2176]{1,0:T(8,128)(2,1)S(1)} %pack_rows.1), channel_id=1, source_target_pairs={{0,4},{1,9},{2,6},{3,11},{4,0},{5,13},{6,2},{7,15},{8,12},{9,1},{1... | collective-permute-start | bytes 522248 | tf_op jit(solution)/shard_map/ppermute | solution.py:40
  12.7 1.6 %collective-permute-start.1 = (bf16[40,2176]{1,0:T(8,128)(2,1)S(1)}, bf16[40,2176]{1,0:T(8,128)(2,1)S(1)}, u32[]{:S(2)}, u32[]{:S(2)}) collective-permute-start(bf16[40,2176]{1,0:T(8,128)(2,1)S(1)} %pack_rows.1), channel_id=1, source_target_pairs={{0,2},{1,129},{2,4},{3,131},{4,6},{5,133},{6,0},{7,135},{8,10},{9,... | collective-permute-start | bytes 522248 | tf_op jit(solution)/shard_map/ppermute | solution.py:40
  14.3 0.4 collective-permute-start
  14.7 2.7 %constant_dynamic-slice_fusion = (bf16[1024,1024]{1,0:T(8,128)(2,1)S(1)}, bf16[1024,1024]{1,0:T(8,128)(2,1)S(1)}) fusion(bf16[2048,1024]{1,0:T(8,128)(2,1)} %param.11, s32[]{:T(128)S(6)} %select_n.23, bf16[1024,2048]{1,0:T(8,128)(2,1)} %param.10), kind=kLoop, calls=%fused_computation.69 | loop fusion | bytes 8388612 | tf_op jit(solution)/shard_map/dynamic_slice | solution.py:268
  17.4 0.1 collective-permute-done.2
  17.5 1.9 %collective-permute-done.1 = bf16[40,2176]{1,0:T(8,128)(2,1)S(1)} collective-permute-done((bf16[40,2176]{1,0:T(8,128)(2,1)S(1)}, bf16[40,2176]{1,0:T(8,128)(2,1)S(1)}, u32[]{:S(2)}, u32[]{:S(2)}) %collective-permute-start.1) | collective-permute-done | bytes 174112 | tf_op jit(solution)/shard_map/ppermute | solution.py:40
  19.4 0.3 collective-permute-done
  19.7 0.1 pad_maximum_fusion.1.refs_0_
  19.8 0.1 collective-permute-start.3
  19.9 2.8 %collective-permute-start.4 = (bf16[160,2176]{1,0:T(8,128)(2,1)S(1)}, bf16[160,2176]{1,0:T(8,128)(2,1)S(1)}, u32[]{:S(2)}, u32[]{:S(2)}) collective-permute-start(bf16[160,2176]{1,0:T(8,128)(2,1)S(1)} %after.3.a_ref), channel_id=1, source_target_pairs={{0,136},{1,7},{2,138},{3,1},{4,140},{5,3},{6,142},{7,5},{8,128},{9... | collective-permute-start | bytes 2088968 | tf_op jit(solution)/shard_map/ppermute | solution.py:40
  22.7 3.1 %chunk_0.1 = (bf16[320,2048]{1,0:T(8,128)(2,1)S(1)}, bf16[320,128]{1,0:T(8,128)(2,1)S(1)}, bf16[320,2048]{1,0:T(8,128)(2,1)S(1)}, bf16[160,1024]{1,0:T(8,128)(2,1)S(1)}, bf16[160,1024]{1,0:T(8,128)(2,1)S(1)}) custom-call(bf16[160,2176]{1,0:T(8,128)(2,1)S(1)} %after.3.a_ref, bf16[160,2176]{1,0:T(8,128)(2,1)S(1)} %collective-permute-done.3.b_ref, ...), custom_call_target="tpu_custom_call" | custom-call | flops 2013265920 | bytes 9437184 | tf_op jit(solution)/shard_map/chunk_0/pallas_call | solution.py:150
  25.8 5.5 %collective-permute-done.4.refs_0_ = bf16[160,2176]{1,0:T(8,128)(2,1)S(1)} collective-permute-done((bf16[160,2176]{1,0:T(8,128)(2,1)S(1)}, bf16[160,2176]{1,0:T(8,128)(2,1)S(1)}, u32[]{:S(2)}, u32[]{:S(2)}) %collective-permute-start.4) | collective-permute-done | bytes 696352 | tf_op jit(solution)/shard_map/ppermute | solution.py:40
  31.2 3.7 %collective-permute-done.5.refs_1_ = bf16[160,2176]{1,0:T(8,128)(2,1)S(1)} collective-permute-done((bf16[160,2176]{1,0:T(8,128)(2,1)S(1)}, bf16[160,2176]{1,0:T(8,128)(2,1)S(1)}, u32[]{:S(2)}, u32[]{:S(2)}) %collective-permute-start.5) | collective-permute-done | bytes 696352 | tf_op jit(solution)/shard_map/ppermute | solution.py:40
  34.9 0.7 collective-permute-start.8
  35.6 1.5 %collective-permute-start.9 = (bf16[80,2176]{1,0:T(8,128)(2,1)S(1)}, bf16[80,2176]{1,0:T(8,128)(2,1)S(1)}, u32[]{:S(2)}, u32[]{:S(2)}) collective-permute-start(bf16[80,2176]{1,0:T(8,128)(2,1)S(1)} %slice.125), channel_id=1, source_target_pairs={{0,128},{1,3},{2,130},{3,5},{4,132},{5,7},{6,134},{7,1},{8,136},{9... | collective-permute-start | bytes 1044488 | tf_op jit(solution)/shard_map/ppermute | solution.py:40
  37.2 3.1 %chunk_1.1 = (bf16[320,2048]{1,0:T(8,128)(2,1)S(1)}, bf16[320,128]{1,0:T(8,128)(2,1)S(1)}, bf16[320,2048]{1,0:T(8,128)(2,1)S(1)}, bf16[160,1024]{1,0:T(8,128)(2,1)S(1)}, bf16[160,1024]{1,0:T(8,128)(2,1)S(1)}) custom-call(bf16[160,2176]{1,0:T(8,128)(2,1)S(1)} %get-tuple-element.32.a_ref, bf16[160,2176]{1,0:T(8,128)(2,1)S(1)} %collective-permute-done.6.b_ref, ...), custom_call_target="tpu_custom_call" | custom-call | flops 2013265920 | bytes 9437184 | tf_op jit(solution)/shard_map/chunk_1/pallas_call | solution.py:150
  40.2 2.1 %collective-permute-done.8.refs_0_ = bf16[80,2176]{1,0:T(8,128)(2,1)S(1)} collective-permute-done((bf16[80,2176]{1,0:T(8,128)(2,1)S(1)}, bf16[80,2176]{1,0:T(8,128)(2,1)S(1)}, u32[]{:S(2)}, u32[]{:S(2)}) %collective-permute-start.8) | collective-permute-done | bytes 348192 | tf_op jit(solution)/shard_map/ppermute | solution.py:40
  42.3 1.9 %collective-permute-done.9.refs_1_ = bf16[80,2176]{1,0:T(8,128)(2,1)S(1)} collective-permute-done((bf16[80,2176]{1,0:T(8,128)(2,1)S(1)}, bf16[80,2176]{1,0:T(8,128)(2,1)S(1)}, u32[]{:S(2)}, u32[]{:S(2)}) %collective-permute-start.9) | collective-permute-done | bytes 348192 | tf_op jit(solution)/shard_map/ppermute | solution.py:40
  44.3 0.2 collective-permute-start.10
  44.5 3.0 %chunk_2.1 = (bf16[320,2048]{1,0:T(8,128)(2,1)S(1)}, bf16[320,128]{1,0:T(8,128)(2,1)S(1)}, bf16[320,2048]{1,0:T(8,128)(2,1)S(1)}, bf16[160,1024]{1,0:T(8,128)(2,1)S(1)}, bf16[160,1024]{1,0:T(8,128)(2,1)S(1)}) custom-call(bf16[160,2176]{1,0:T(8,128)(2,1)S(1)} %get-tuple-element.34.a_ref, bf16[160,2176]{1,0:T(8,128)(2,1)S(1)} %collective-permute-done.7.b_ref, ...), custom_call_target="tpu_custom_call" | custom-call | flops 2013265920 | bytes 9437184 | tf_op jit(solution)/shard_map/chunk_2/pallas_call | solution.py:150
  47.5 3.0 %chunk_3.1 = (bf16[320,2048]{1,0:T(8,128)(2,1)S(1)}, bf16[320,128]{1,0:T(8,128)(2,1)S(1)}, bf16[320,2048]{1,0:T(8,128)(2,1)S(1)}, bf16[160,1024]{1,0:T(8,128)(2,1)S(1)}, bf16[160,1024]{1,0:T(8,128)(2,1)S(1)}) custom-call(bf16[160,2176]{1,0:T(8,128)(2,1)S(1)} %constant_dynamic-update-slice_fusion.a_ref, bf16[160,2176]{1,0:T(8,128)(2,1)S(1)} %collective-permute-done.10.b_ref, ...), custom_call_target="tpu_custom_call" | custom-call | flops 2013265920 | bytes 9437184 | tf_op jit(solution)/shard_map/chunk_3/pallas_call | solution.py:150
  50.6 9.7 %weight_grads.1 = (bf16[8,2,2,64,1024]{4,3,2,1,0:T(8,128)(2,1)}, f32[8,1024]{1,0:T(8,128)S(1)}, f32[40,128]{1,0:T(8,128)S(1)}) custom-call(bf16[320,128]{1,0:T(8,128)(2,1)S(1)} %get-tuple-element.31.refs_2_.refs_0_, bf16[320,128]{1,0:T(8,128)(2,1)S(1)} %get-tuple-element.33.refs_2_.refs_1_, bf16[320,128]{1,0:T(8,128)(2,1)S(1)} %get-tuple-element.35.refs_2_, ...), custom_call_target="tpu_custom_call" | custom-call | flops 5368709120 | bytes 25165824 | tf_op jit(solution)/shard_map/weight_grads/pallas_call | solution.py:218
  60.3 0.1 pad_maximum_fusion
  60.4 0.5 collective-permute-start.11
  60.9 0.3 collective-permute-start.12
  61.2 2.4 %collective-permute-done.12 = f32[8,1024]{1,0:T(8,128)S(1)} collective-permute-done((f32[8,1024]{1,0:T(8,128)S(1)}, f32[8,1024]{1,0:T(8,128)S(1)}, u32[]{:S(2)}, u32[]{:S(2)}) %collective-permute-start.12) | collective-permute-done | bytes 32800 | tf_op jit(solution)/shard_map/ppermute | solution.py:40
  63.6 0.6 add_convert_fusion
  64.3 0.1 fusion.32
  64.3 1.0 pad_maximum_fusion.4
  65.3 0.4 collective-permute-start.15
  65.7 2.5 %collective-permute-start.14 = (bf16[168,1024]{1,0:T(8,128)(2,1)}, bf16[168,1024]{1,0:T(8,128)(2,1)}, u32[]{:S(2)}, u32[]{:S(2)}) collective-permute-start(bf16[168,1024]{1,0:T(8,128)(2,1)} %get-tuple-element.76), channel_id=1, source_target_pairs={{0,136},{1,7},{2,138},{3,1},{4,140},{5,3},{6,142},{7,5},{8,128},{9... | collective-permute-start | bytes 1032200 | tf_op jit(solution)/shard_map/ppermute | solution.py:40
  68.3 0.1 fusion.10
  68.4 6.0 %collective-permute-done.15 = bf16[168,1024]{1,0:T(8,128)(2,1)S(1)} collective-permute-done((bf16[168,1024]{1,0:T(8,128)(2,1)}, bf16[168,1024]{1,0:T(8,128)(2,1)S(1)}, u32[]{:S(2)}, u32[]{:S(2)}) %collective-permute-start.15) | collective-permute-done | bytes 344096 | tf_op jit(solution)/shard_map/ppermute | solution.py:40
  74.4 1.2 collective-permute-done.14
  75.6 2.5 %collective-permute-done.13 = bf16[168,1024]{1,0:T(8,128)(2,1)} collective-permute-done((bf16[168,1024]{1,0:T(8,128)(2,1)S(1)}, bf16[168,1024]{1,0:T(8,128)(2,1)}, u32[]{:S(2)}, u32[]{:S(2)}) %collective-permute-start.13) | collective-permute-done | bytes 344096 | tf_op jit(solution)/shard_map/ppermute | solution.py:40
  78.1 0.8 fusion.29
  78.9 1.3 add_convert_fusion.1
  80.3 2.9 %collective-permute-start.18 = (bf16[48,1024]{1,0:T(8,128)(2,1)S(1)}, bf16[48,1024]{1,0:T(8,128)(2,1)S(1)}, u32[]{:S(2)}, u32[]{:S(2)}) collective-permute-start(bf16[48,1024]{1,0:T(8,128)(2,1)S(1)} %get-tuple-element.74), channel_id=1, source_target_pairs={{0,4},{1,9},{2,6},{3,11},{4,0},{5,13},{6,2},{7,15},{8,12},{9,1},{1... | collective-permute-start | bytes 294920 | tf_op jit(solution)/shard_map/ppermute | solution.py:40
  83.2 0.2 collective-permute-start.17
  83.4 1.8 %collective-permute-start.16 = (bf16[48,1024]{1,0:T(8,128)(2,1)S(1)}, bf16[48,1024]{1,0:T(8,128)(2,1)S(1)}, u32[]{:S(2)}, u32[]{:S(2)}) collective-permute-start(bf16[48,1024]{1,0:T(8,128)(2,1)S(1)} %get-tuple-element.72), channel_id=1, source_target_pairs={{0,2},{1,129},{2,4},{3,131},{4,6},{5,133},{6,0},{7,135},{8,10},{9,... | collective-permute-start | bytes 294920 | tf_op jit(solution)/shard_map/ppermute | solution.py:40
  85.2 0.1 slice_reduce_fusion
  85.3 1.2 collective-permute-done.18
  86.5 1.3 collective-permute-done.17
  87.8 0.2 collective-permute-done.16
  88.1 2.0 %collective-permute-start.20 = (f32[8,128]{1,0:T(8,128)S(1)}, f32[8,128]{1,0:T(8,128)S(1)}, u32[]{:S(2)}, u32[]{:S(2)}) collective-permute-start(f32[8,128]{1,0:T(8,128)S(1)} %bitcast.24), channel_id=1, source_target_pairs={{0,16},{1,17},{2,18},{3,19},{4,20},{5,21},{6,22},{7,23},{8,24},{9,... | collective-permute-start | bytes 12296 | tf_op jit(solution)/shard_map/ppermute | solution.py:40
  90.1 0.2 fusion.5
  90.3 1.7 %collective-permute-done.20 = f32[8,128]{1,0:T(8,128)S(1)} collective-permute-done((f32[8,128]{1,0:T(8,128)S(1)}, f32[8,128]{1,0:T(8,128)S(1)}, u32[]{:S(2)}, u32[]{:S(2)}) %collective-permute-start.20) | collective-permute-done | bytes 4128 | tf_op jit(solution)/shard_map/ppermute | solution.py:40
  92.0 3.2 %collective-permute-start.21 = (f32[8,128]{1,0:T(8,128)S(1)}, f32[8,128]{1,0:T(8,128)S(1)}, u32[]{:S(2)}, u32[]{:S(2)}) collective-permute-start(f32[8,128]{1,0:T(8,128)S(1)} %add.168), channel_id=1, source_target_pairs={{0,32},{1,33},{2,34},{3,35},{4,36},{5,37},{6,38},{7,39},{8,40},{9,... | collective-permute-start | bytes 12296 | tf_op jit(solution)/shard_map/ppermute | solution.py:40
  95.2 1.8 %collective-permute-done.21 = f32[8,128]{1,0:T(8,128)S(1)} collective-permute-done((f32[8,128]{1,0:T(8,128)S(1)}, f32[8,128]{1,0:T(8,128)S(1)}, u32[]{:S(2)}, u32[]{:S(2)}) %collective-permute-start.21) | collective-permute-done | bytes 4128 | tf_op jit(solution)/shard_map/ppermute | solution.py:40
  97.0 7.0 %collective-permute-start.22 = (f32[8,128]{1,0:T(8,128)S(1)}, f32[8,128]{1,0:T(8,128)S(1)}, u32[]{:S(2)}, u32[]{:S(2)}) collective-permute-start(f32[8,128]{1,0:T(8,128)S(1)} %add.169), channel_id=1, source_target_pairs={{0,64},{1,65},{2,66},{3,67},{4,68},{5,69},{6,70},{7,71},{8,72},{9,... | collective-permute-start | bytes 12296 | tf_op jit(solution)/shard_map/ppermute | solution.py:40
  104.0 13.0 %reduce-scatter.2.cloned.1.call-done = bf16[256,1024]{1,0:T(8,128)(2,1)} async-done(((bf16[2048,1024]{1,0:T(8,128)(2,1)}), bf16[256,1024]{1,0:T(8,128)(2,1)}) %reduce-scatter.2.cloned.1.call-update) | async-done | bytes 524304 | tf_op jit(solution)/shard_map/reduce_scatter | solution.py:290
  117.0 1.0 dynamic-slice_bitcast_fusion
  118.0 1.6 %collective-permute-start.19 = (bf16[2,64,1024]{2,1,0:T(8,128)(2,1)S(1)}, bf16[2,64,1024]{2,1,0:T(8,128)(2,1)S(1)}, u32[]{:S(2)}, u32[]{:S(2)}) collective-permute-start(bf16[2,64,1024]{2,1,0:T(8,128)(2,1)S(1)} %dynamic-slice_bitcast_fusion), channel_id=1, source_target_pairs={{0,128},{1,129},{2,130},{3,131},{4,132},{5,133},{6,134},{7,135},{8... | collective-permute-start | bytes 786440 | tf_op jit(solution)/shard_map/ppermute | solution.py:40
  119.5 0.8 fusion.9
  120.3 0.6 bitcast_divide_fusion
  120.9 5.3 %collective-permute-done.19 = bf16[2,64,1024]{2,1,0:T(8,128)(2,1)S(1)} collective-permute-done((bf16[2,64,1024]{2,1,0:T(8,128)(2,1)S(1)}, bf16[2,64,1024]{2,1,0:T(8,128)(2,1)S(1)}, u32[]{:S(2)}, u32[]{:S(2)}) %collective-permute-start.19) | collective-permute-done | bytes 262176 | tf_op jit(solution)/shard_map/ppermute | solution.py:40
  126.2 1.0 bitcast_select_fusion
  127.2 0.8 fusion.2
  (41 shorter events, 0.3 us)
Async XLA Ops:
  7.2 109.8 %reduce-scatter.2.cloned.1.call-start = ((), (), s32[]{:S(2)}) async-start(), calls=%async_computation.1 | async-start | bytes 4718592 | tf_op jit(solution)/shard_map/reduce_scatter | solution.py:290
  7.2 0.9 copy-start
  8.1 0.9 copy-start.2
  9.0 0.7 copy-start.4
  9.7 0.7 copy-start.6
  10.4 7.0 %collective-permute-start.2 = (bf16[40,2176]{1,0:T(8,128)(2,1)S(1)}, bf16[40,2176]{1,0:T(8,128)(2,1)S(1)}, u32[]{:S(2)}, u32[]{:S(2)}) collective-permute-start(bf16[40,2176]{1,0:T(8,128)(2,1)S(1)} %pack_rows.1), channel_id=1, source_target_pairs={{0,4},{1,9},{2,6},{3,11},{4,0},{5,13},{6,2},{7,15},{8,12},{9,1},{1... | collective-permute-start | bytes 522248 | tf_op jit(solution)/shard_map/ppermute | solution.py:40
  12.7 6.7 %collective-permute-start.1 = (bf16[40,2176]{1,0:T(8,128)(2,1)S(1)}, bf16[40,2176]{1,0:T(8,128)(2,1)S(1)}, u32[]{:S(2)}, u32[]{:S(2)}) collective-permute-start(bf16[40,2176]{1,0:T(8,128)(2,1)S(1)} %pack_rows.1), channel_id=1, source_target_pairs={{0,2},{1,129},{2,4},{3,131},{4,6},{5,133},{6,0},{7,135},{8,10},{9,... | collective-permute-start | bytes 522248 | tf_op jit(solution)/shard_map/ppermute | solution.py:40
  14.3 5.4 %collective-permute-start = (bf16[40,2176]{1,0:T(8,128)(2,1)S(1)}, bf16[40,2176]{1,0:T(8,128)(2,1)S(1)}, u32[]{:S(2)}, u32[]{:S(2)}) collective-permute-start(bf16[40,2176]{1,0:T(8,128)(2,1)S(1)} %pack_rows.1), channel_id=1, source_target_pairs={{0,6},{1,137},{2,0},{3,139},{4,2},{5,141},{6,4},{7,143},{8,14},{9,... | collective-permute-start | bytes 522248 | tf_op jit(solution)/shard_map/ppermute | solution.py:40
  19.8 2.9 %collective-permute-start.3 = (bf16[160,2176]{1,0:T(8,128)(2,1)S(1)}, bf16[160,2176]{1,0:T(8,128)(2,1)S(1)}, u32[]{:S(2)}, u32[]{:S(2)}) collective-permute-start(bf16[160,2176]{1,0:T(8,128)(2,1)S(1)} %after.3.a_ref), channel_id=1, source_target_pairs={{0,1},{1,0},{2,3},{3,2},{4,5},{5,4},{6,7},{7,6},{8,9},{9,8},{10,11... | collective-permute-start | bytes 2088968 | tf_op jit(solution)/shard_map/ppermute | solution.py:40
  19.9 11.4 %collective-permute-start.4 = (bf16[160,2176]{1,0:T(8,128)(2,1)S(1)}, bf16[160,2176]{1,0:T(8,128)(2,1)S(1)}, u32[]{:S(2)}, u32[]{:S(2)}) collective-permute-start(bf16[160,2176]{1,0:T(8,128)(2,1)S(1)} %after.3.a_ref), channel_id=1, source_target_pairs={{0,136},{1,7},{2,138},{3,1},{4,140},{5,3},{6,142},{7,5},{8,128},{9... | collective-permute-start | bytes 2088968 | tf_op jit(solution)/shard_map/ppermute | solution.py:40
  22.7 12.2 %collective-permute-start.5 = (bf16[160,2176]{1,0:T(8,128)(2,1)S(1)}, bf16[160,2176]{1,0:T(8,128)(2,1)S(1)}, u32[]{:S(2)}, u32[]{:S(2)}) collective-permute-start(bf16[160,2176]{1,0:T(8,128)(2,1)S(1)} %after.3.a_ref), channel_id=1, source_target_pairs={{0,128},{1,3},{2,130},{3,5},{4,132},{5,7},{6,134},{7,1},{8,136},{9... | collective-permute-start | bytes 2088968 | tf_op jit(solution)/shard_map/ppermute | solution.py:40
  34.9 2.2 %collective-permute-start.6 = (bf16[160,2176]{1,0:T(8,128)(2,1)S(1)}, bf16[160,2176]{1,0:T(8,128)(2,1)S(1)}, u32[]{:S(2)}, u32[]{:S(2)}) collective-permute-start(bf16[160,2176]{1,0:T(8,128)(2,1)S(1)} %get-tuple-element.32.a_ref), channel_id=1, source_target_pairs={{0,1},{1,0},{2,3},{3,2},{4,5},{5,4},{6,7},{7,6},{8,9},{9,8},{10,11... | collective-permute-start | bytes 2088968 | tf_op jit(solution)/shard_map/ppermute | solution.py:40
  34.9 7.4 %collective-permute-start.8 = (bf16[80,2176]{1,0:T(8,128)(2,1)S(1)}, bf16[80,2176]{1,0:T(8,128)(2,1)S(1)}, u32[]{:S(2)}, u32[]{:S(2)}) collective-permute-start(bf16[80,2176]{1,0:T(8,128)(2,1)S(1)} %slice.124), channel_id=1, source_target_pairs={{0,136},{1,7},{2,138},{3,1},{4,140},{5,3},{6,142},{7,5},{8,128},{9... | collective-permute-start | bytes 1044488 | tf_op jit(solution)/shard_map/ppermute | solution.py:40
  35.6 8.6 %collective-permute-start.9 = (bf16[80,2176]{1,0:T(8,128)(2,1)S(1)}, bf16[80,2176]{1,0:T(8,128)(2,1)S(1)}, u32[]{:S(2)}, u32[]{:S(2)}) collective-permute-start(bf16[80,2176]{1,0:T(8,128)(2,1)S(1)} %slice.125), channel_id=1, source_target_pairs={{0,128},{1,3},{2,130},{3,5},{4,132},{5,7},{6,134},{7,1},{8,136},{9... | collective-permute-start | bytes 1044488 | tf_op jit(solution)/shard_map/ppermute | solution.py:40
  37.2 7.3 %collective-permute-start.7 = (bf16[160,2176]{1,0:T(8,128)(2,1)S(1)}, bf16[160,2176]{1,0:T(8,128)(2,1)S(1)}, u32[]{:S(2)}, u32[]{:S(2)}) collective-permute-start(bf16[160,2176]{1,0:T(8,128)(2,1)S(1)} %get-tuple-element.34.a_ref), channel_id=1, source_target_pairs={{0,1},{1,0},{2,3},{3,2},{4,5},{5,4},{6,7},{7,6},{8,9},{9,8},{10,11... | collective-permute-start | bytes 2088968 | tf_op jit(solution)/shard_map/ppermute | solution.py:40
  44.3 3.2 %collective-permute-start.10 = (bf16[160,2176]{1,0:T(8,128)(2,1)S(1)}, bf16[160,2176]{1,0:T(8,128)(2,1)S(1)}, u32[]{:S(2)}, u32[]{:S(2)}) collective-permute-start(bf16[160,2176]{1,0:T(8,128)(2,1)S(1)} %constant_dynamic-update-slice_fusion.a_ref), channel_id=1, source_target_pairs={{0,1},{1,0},{2,3},{3,2},{4,5},{5,4},{6,7},{7,6},{8,9},{9,8},{10,11... | collective-permute-start | bytes 2088968 | tf_op jit(solution)/shard_map/ppermute | solution.py:40
  60.4 3.2 %collective-permute-start.11 = (bf16[640,1024]{1,0:T(8,128)(2,1)S(1)}, bf16[640,1024]{1,0:T(8,128)(2,1)S(1)}, u32[]{:S(2)}, u32[]{:S(2)}) collective-permute-start(bf16[640,1024]{1,0:T(8,128)(2,1)S(1)} %pad_maximum_fusion), channel_id=1, source_target_pairs={{0,1},{1,0},{2,3},{3,2},{4,5},{5,4},{6,7},{7,6},{8,9},{9,8},{10,11... | collective-permute-start | bytes 3932168 | tf_op jit(solution)/shard_map/ppermute | solution.py:40
  60.9 2.7 %collective-permute-start.12 = (f32[8,1024]{1,0:T(8,128)S(1)}, f32[8,1024]{1,0:T(8,128)S(1)}, u32[]{:S(2)}, u32[]{:S(2)}) collective-permute-start(f32[8,1024]{1,0:T(8,128)S(1)} %get-tuple-element.56), channel_id=1, source_target_pairs={{0,1},{1,0},{2,3},{3,2},{4,5},{5,4},{6,7},{7,6},{8,9},{9,8},{10,11... | collective-permute-start | bytes 98312 | tf_op jit(solution)/shard_map/ppermute | solution.py:40
  64.3 3.9 %copy-start.5 = (bf16[1024]{0:T(1024)(128)(2,1)S(1)}, bf16[1024]{0:T(1024)(128)(2,1)}, u32[]{:S(2)}) copy-start(bf16[1024]{0:T(1024)(128)(2,1)} %gain_ref.1) | copy-start | bytes 6148
  64.3 3.9 %copy-start.1 = (bf16[40,1024]{1,0:T(8,128)(2,1)S(1)}, bf16[40,1024]{1,0:T(8,128)(2,1)}, u32[]{:S(2)}) copy-start(bf16[40,1024]{1,0:T(8,128)(2,1)} %x_ref.1) | copy-start | bytes 245764
  65.3 9.1 %collective-permute-start.15 = (bf16[168,1024]{1,0:T(8,128)(2,1)}, bf16[168,1024]{1,0:T(8,128)(2,1)S(1)}, u32[]{:S(2)}, u32[]{:S(2)}) collective-permute-start(bf16[168,1024]{1,0:T(8,128)(2,1)} %get-tuple-element.77), channel_id=1, source_target_pairs={{0,8},{1,5},{2,10},{3,7},{4,12},{5,1},{6,14},{7,3},{8,0},{9,13},{1... | collective-permute-start | bytes 1032200 | tf_op jit(solution)/shard_map/ppermute | solution.py:40
  65.7 9.9 %collective-permute-start.14 = (bf16[168,1024]{1,0:T(8,128)(2,1)}, bf16[168,1024]{1,0:T(8,128)(2,1)}, u32[]{:S(2)}, u32[]{:S(2)}) collective-permute-start(bf16[168,1024]{1,0:T(8,128)(2,1)} %get-tuple-element.76), channel_id=1, source_target_pairs={{0,136},{1,7},{2,138},{3,1},{4,140},{5,3},{6,142},{7,5},{8,128},{9... | collective-permute-start | bytes 1032200 | tf_op jit(solution)/shard_map/ppermute | solution.py:40
  68.2 9.8 %collective-permute-start.13 = (bf16[168,1024]{1,0:T(8,128)(2,1)S(1)}, bf16[168,1024]{1,0:T(8,128)(2,1)}, u32[]{:S(2)}, u32[]{:S(2)}) collective-permute-start(bf16[168,1024]{1,0:T(8,128)(2,1)S(1)} %get-tuple-element.75), channel_id=1, source_target_pairs={{0,128},{1,3},{2,130},{3,5},{4,132},{5,7},{6,134},{7,1},{8,136},{9... | collective-permute-start | bytes 1032200 | tf_op jit(solution)/shard_map/ppermute | solution.py:40
  80.2 39.3 %copy-start.3 = (bf16[40,1024]{1,0:T(8,128)(2,1)S(1)}, bf16[40,1024]{1,0:T(8,128)(2,1)}, u32[]{:S(2)}) copy-start(bf16[40,1024]{1,0:T(8,128)(2,1)} %cot_ref.1) | copy-start | bytes 245764
  80.3 6.2 %collective-permute-start.18 = (bf16[48,1024]{1,0:T(8,128)(2,1)S(1)}, bf16[48,1024]{1,0:T(8,128)(2,1)S(1)}, u32[]{:S(2)}, u32[]{:S(2)}) collective-permute-start(bf16[48,1024]{1,0:T(8,128)(2,1)S(1)} %get-tuple-element.74), channel_id=1, source_target_pairs={{0,4},{1,9},{2,6},{3,11},{4,0},{5,13},{6,2},{7,15},{8,12},{9,1},{1... | collective-permute-start | bytes 294920 | tf_op jit(solution)/shard_map/ppermute | solution.py:40
  83.2 4.6 %collective-permute-start.17 = (bf16[48,1024]{1,0:T(8,128)(2,1)S(1)}, bf16[48,1024]{1,0:T(8,128)(2,1)S(1)}, u32[]{:S(2)}, u32[]{:S(2)}) collective-permute-start(bf16[48,1024]{1,0:T(8,128)(2,1)S(1)} %get-tuple-element.73), channel_id=1, source_target_pairs={{0,6},{1,137},{2,0},{3,139},{4,2},{5,141},{6,4},{7,143},{8,14},{9,... | collective-permute-start | bytes 294920 | tf_op jit(solution)/shard_map/ppermute | solution.py:40
  83.4 4.6 %collective-permute-start.16 = (bf16[48,1024]{1,0:T(8,128)(2,1)S(1)}, bf16[48,1024]{1,0:T(8,128)(2,1)S(1)}, u32[]{:S(2)}, u32[]{:S(2)}) collective-permute-start(bf16[48,1024]{1,0:T(8,128)(2,1)S(1)} %get-tuple-element.72), channel_id=1, source_target_pairs={{0,2},{1,129},{2,4},{3,131},{4,6},{5,133},{6,0},{7,135},{8,10},{9,... | collective-permute-start | bytes 294920 | tf_op jit(solution)/shard_map/ppermute | solution.py:40
  88.1 3.9 %collective-permute-start.20 = (f32[8,128]{1,0:T(8,128)S(1)}, f32[8,128]{1,0:T(8,128)S(1)}, u32[]{:S(2)}, u32[]{:S(2)}) collective-permute-start(f32[8,128]{1,0:T(8,128)S(1)} %bitcast.24), channel_id=1, source_target_pairs={{0,16},{1,17},{2,18},{3,19},{4,20},{5,21},{6,22},{7,23},{8,24},{9,... | collective-permute-start | bytes 12296 | tf_op jit(solution)/shard_map/ppermute | solution.py:40
  92.0 5.0 %collective-permute-start.21 = (f32[8,128]{1,0:T(8,128)S(1)}, f32[8,128]{1,0:T(8,128)S(1)}, u32[]{:S(2)}, u32[]{:S(2)}) collective-permute-start(f32[8,128]{1,0:T(8,128)S(1)} %add.168), channel_id=1, source_target_pairs={{0,32},{1,33},{2,34},{3,35},{4,36},{5,37},{6,38},{7,39},{8,40},{9,... | collective-permute-start | bytes 12296 | tf_op jit(solution)/shard_map/ppermute | solution.py:40
  97.0 23.3 %collective-permute-start.22 = (f32[8,128]{1,0:T(8,128)S(1)}, f32[8,128]{1,0:T(8,128)S(1)}, u32[]{:S(2)}, u32[]{:S(2)}) collective-permute-start(f32[8,128]{1,0:T(8,128)S(1)} %add.169), channel_id=1, source_target_pairs={{0,64},{1,65},{2,66},{3,67},{4,68},{5,69},{6,70},{7,71},{8,72},{9,... | collective-permute-start | bytes 12296 | tf_op jit(solution)/shard_map/ppermute | solution.py:40
  118.0 8.2 %collective-permute-start.19 = (bf16[2,64,1024]{2,1,0:T(8,128)(2,1)S(1)}, bf16[2,64,1024]{2,1,0:T(8,128)(2,1)S(1)}, u32[]{:S(2)}, u32[]{:S(2)}) collective-permute-start(bf16[2,64,1024]{2,1,0:T(8,128)(2,1)S(1)} %dynamic-slice_bitcast_fusion), channel_id=1, source_target_pairs={{0,128},{1,129},{2,130},{3,131},{4,132},{5,133},{6,134},{7,135},{8... | collective-permute-start | bytes 786440 | tf_op jit(solution)/shard_map/ppermute | solution.py:40
Sparse Core Ops, SparseCore 0:
  60.4 56.5 reduce-scatter.1
